TPU v7x, 256 devices: a whole 4x4x8 slice. The times are simulated.
256 devices in a mesh: role: 2 (over core), grp: 8 (over z), tp: 16 (over y, x).
Axes of the slice: x: 4, y: 4, z: 8, core: 2. Of those that a mesh axis runs over, the one named last changes fastest.
Arguments:
- queries: bfloat16 [2048, 3072], P(('grp', 'tp')), may hold values from -96 to 96
- cached_keys: bfloat16 [2048, 128, 512], P(('grp', 'tp')), may hold values from -4 to 4
- cached_values: bfloat16 [2048, 128, 512], P(('grp', 'tp')), may hold values from -6 to 6
- lengths: int32 [2048], P(('grp', 'tp')), may hold values from 2 to 128, as said below
- norm_gain: float32 [3072], replicated, may hold values from 0.25 to 1.75
- expert_ids: int32 [2048, 2], P(('grp', 'tp')), may hold values from 0 to 7, all different within a row; in each aligned block of 16 rows (0 to 15, 16 to 31, ...) at most 8 rows name the same one
- gates: float32 [2048, 2], P(('grp', 'tp')), may hold values from 0.1 to 1
- gate_proj: bfloat16 [8, 3072, 8192], P('grp', None, 'tp'), may hold values from -0.109375 to 0.109375
- up_proj: bfloat16 [8, 3072, 8192], P('grp', None, 'tp'), may hold values from -0.109375 to 0.109375
- down_proj: bfloat16 [8, 8192, 3072], P('grp', 'tp'), may hold values from -0.0625 to 0.0625
Outputs:
- mixed: bfloat16 [2048, 3072], P(('grp', 'tp'), 'role')
Inputs may be any that keep to these rules, and one draw needn't show every extreme that they name: `expert_ids`: each row names two different experts. Among the 16 rows of one attention device (aligned blocks) no expert is named by more than 8 rows, and some block has an expert named by exactly 8 rows. `lengths`: some request has all 128 positions valid.
All inputs are finite; a program needn't handle non-finite values.
Results may differ from a plain program's by a relative error of at most 0.02.
Values may be sent and summed in bfloat16 or wider, within the bound.
A program may use at most 64 MiB of HBM per device.

v0:
```python
import math

import jax
import jax.numpy as jnp
from jax import lax
from jax.sharding import PartitionSpec as P

HEAD_WIDTH = 128
QUERY_HEADS = 24
KEY_VALUE_HEADS = 4
MODEL_WIDTH = 3072
MOST = 8


def shifted(x, axis, by):
    peers = lax.axis_size(axis)
    pairs = [(i, i + by) for i in range(peers) if 0 <= i + by < peers]
    return lax.ppermute(x, axis, pairs)


def attend(queries, cached_keys, cached_values, lengths, norm_gain):
    count_of_rows = queries.shape[0]
    cache_positions = cached_keys.shape[1]
    heads_of_queries = queries.reshape(
        count_of_rows, KEY_VALUE_HEADS, QUERY_HEADS // KEY_VALUE_HEADS, HEAD_WIDTH
    )
    heads_of_keys = cached_keys.reshape(count_of_rows, cache_positions, KEY_VALUE_HEADS, HEAD_WIDTH)
    heads_of_values = cached_values.reshape(
        count_of_rows, cache_positions, KEY_VALUE_HEADS, HEAD_WIDTH
    )
    scores = jnp.einsum(
        "rjgd,rcjd->rjgc", heads_of_queries, heads_of_keys, preferred_element_type=jnp.float32
    ) / math.sqrt(HEAD_WIDTH)
    valid = jnp.arange(cache_positions)[None, :] < lengths[:, None]
    scores = jnp.where(valid[:, None, None, :], scores, -jnp.inf)
    score_peak = jnp.max(scores, axis=-1, keepdims=True)
    raised = jnp.exp(scores - score_peak)
    weights = (raised / jnp.sum(raised, axis=-1, keepdims=True)).astype(jnp.bfloat16)
    context_mixed = jnp.einsum(
        "rjgc,rcjd->rjgd", weights, heads_of_values, preferred_element_type=jnp.float32
    )
    context_mixed = context_mixed.reshape(count_of_rows, QUERY_HEADS * HEAD_WIDTH)
    mean_square = jnp.mean(context_mixed * context_mixed, axis=-1, keepdims=True)
    return (context_mixed * lax.rsqrt(mean_square + 1e-05) * norm_gain).astype(jnp.bfloat16)


def slot_table(expert_ids, expert_count):
    expert_hit = jnp.any(
        expert_ids[:, :, None] == jnp.arange(expert_count)[None, None, :], axis=1
    ).astype(jnp.int32)
    slot_rank = jnp.cumsum(expert_hit, axis=0) - expert_hit
    return (expert_hit[:, :, None] == 1) & (
        slot_rank[:, :, None] == jnp.arange(MOST)[None, None, :]
    )


def local(
    queries,
    cached_keys,
    cached_values,
    lengths,
    norm_gain,
    expert_ids,
    gates,
    gate_proj,
    up_proj,
    down_proj,
):
    request_count = queries.shape[0]
    expert_count = lax.axis_size("grp")
    is_attention = lax.axis_index("role") == 0
    half_width = MODEL_WIDTH // lax.axis_size("role")
    first_column = lax.axis_index("role") * half_width

    def attention_side():
        return attend(queries, cached_keys, cached_values, lengths, norm_gain)

    def expert_side():
        return jnp.zeros((request_count, MODEL_WIDTH), jnp.bfloat16)

    expert_in = lax.cond(is_attention, attention_side, expert_side)
    placed = slot_table(expert_ids, expert_count)
    outgoing = jnp.einsum(
        "res,rd->esd", placed.astype(jnp.bfloat16), expert_in, preferred_element_type=jnp.float32
    ).astype(jnp.bfloat16)
    arrived = shifted(outgoing, "role", 1)
    grouped = lax.all_to_all(arrived, "grp", split_axis=0, concat_axis=0, tiled=True)
    tok_rows = grouped.reshape(expert_count * MOST, MODEL_WIDTH)
    gate_weight = gate_proj[0]
    up_weight = up_proj[0]
    down_weight = down_proj[0]
    shard_rows = lax.all_gather(tok_rows, "tp", axis=0, tiled=True)

    def compute():
        gate_part = jnp.dot(shard_rows, gate_weight, preferred_element_type=jnp.float32)
        up_part = jnp.dot(shard_rows, up_weight, preferred_element_type=jnp.float32)
        return (jax.nn.silu(gate_part) * up_part).astype(jnp.bfloat16)

    def skipped():
        return jnp.zeros((shard_rows.shape[0], gate_weight.shape[1]), jnp.bfloat16)

    hidden = lax.cond(is_attention, skipped, compute)
    block_rows = expert_count * MOST
    partial_sums = jnp.dot(hidden, down_weight, preferred_element_type=jnp.float32)
    summed = lax.psum(partial_sums.astype(jnp.bfloat16), "tp").astype(jnp.float32)
    own_sums = lax.dynamic_slice_in_dim(summed, lax.axis_index("tp") * block_rows, block_rows, 0)
    expert_out = own_sums.astype(jnp.bfloat16).reshape(expert_count, MOST, MODEL_WIDTH)
    returned = lax.all_to_all(expert_out, "grp", split_axis=0, concat_axis=0, tiled=True)
    chosen = (expert_ids[:, :, None] == jnp.arange(expert_count)[None, None, :]).astype(jnp.float32)
    per_expert = jnp.einsum("rk,rke->re", gates, chosen, precision=lax.Precision.HIGHEST)
    mix_weight = per_expert[:, :, None] * placed.astype(jnp.float32)
    came_back = shifted(returned, "role", -1)
    source_rows = jnp.where(is_attention, came_back, returned)
    own_rows = lax.dynamic_slice_in_dim(source_rows, first_column, half_width, 2)
    mixed = jnp.einsum(
        "res,esd->rd", mix_weight, own_rows.astype(jnp.float32), precision=lax.Precision.HIGHEST
    ).astype(jnp.bfloat16)
    return mixed


def solution(mesh):
    placed = (
        P(("grp", "tp"), None),
        P(("grp", "tp"), None, None),
        P(("grp", "tp"), None, None),
        P(("grp", "tp")),
        P(),
        P(("grp", "tp"), None),
        P(("grp", "tp"), None),
        P("grp", None, "tp"),
        P("grp", None, "tp"),
        P("grp", "tp", None),
    )
    return jax.shard_map(
        local, mesh=mesh, in_specs=placed, out_specs=P(("grp", "tp"), "role"), check_vma=False
    )
```

profile of v0, /device:TPU:1, one launch (start us, length us, event | category | flops | bytes accessed | tf_op | source)
XLA Modules:
  0.0 293.4 jit_solution(7452426732189169580)
XLA Ops:
  6.5 0.0 copy-start
  6.5 0.0 all-gather.2.cloned.1.call-start
  6.5 0.8 fusion.38
  7.4 0.1 copy.30
  7.5 0.1 copy.32
  7.6 0.1 copy.31
  7.7 0.6 conditional.2
  7.7 0.6 broadcast.45
  8.3 1.1 convolution_convert_fusion.1
  9.4 1.3 collective-permute-start
  10.7 13.5 %collective-permute-done = bf16[8,8,3072]{2,1,0:T(8,128)(2,1)S(1)} collective-permute-done((bf16[8,8,3072]{2,1,0:T(8,128)(2,1)S(1)}, bf16[8,8,3072]{2,1,0:T(8,128)(2,1)S(1)}, u32[]{:S(2)}, u32[]{:S(2)}) %collective-permute-start) | collective-permute-done | bytes 393248 | tf_op jit(solution)/shard_map/ppermute | solution.py:18
  24.3 21.4 %all_to_all.10 = bf16[8,8,3072]{2,1,0:T(8,128)(2,1)} all-to-all(bf16[8,8,3072]{2,1,0:T(8,128)(2,1)S(1)} %collective-permute-done), channel_id=1, replica_groups=mesh['role'=2,'grp'=8,'tp'=16] {'grp'}, dimensions={0} | all-to-all | bytes 786432 | tf_op jit(solution)/shard_map/all_to_all | solution.py:87
  45.7 0.0 all-gather.2.cloned.1.call-update
  45.7 0.0 all-reduce.2.cloned.1.call-start
  45.8 62.7 %all-gather.2.cloned.1.call-done = bf16[1024,3072]{1,0:T(8,128)(2,1)} async-done(((bf16[64,3072]{1,0:T(8,128)(2,1)}), bf16[1024,3072]{1,0:T(8,128)(2,1)}) %all-gather.2.cloned.1.call-update) | async-done | bytes 6291472 | tf_op jit(solution)/shard_map/all_gather | solution.py:92
  108.5 11.3 %conditional.3 = (bf16[1024,512]{1,0:T(8,128)(2,1)}) conditional(s32[]{:T(128)} %convert_element_type.47, (bf16[1,3072,512]{2,1,0:T(8,128)(2,1)}, bf16[1024,3072]{1,0:T(8,128)(2,1)}, bf16[1,3072,512]{2,1,0:T(8,128)(2,1)}) %tuple.19, () %tuple.20), branch_computations={%region_7.8_spmd, %region_8.9_spmd} | conditional | flops 6445596672 | bytes 61866048 | solution.py:102
  108.5 0.0 copy-start.4
  108.5 6.6 %fusion.16 = f32[1024,512]{1,0:T(8,128)S(1)} fusion(bf16[1024,3072]{1,0:T(8,128)(2,1)} %get-tuple-element.34, bf16[1,3072,512]{2,1,0:T(8,128)(2,1)} %get-tuple-element.50), kind=kOutput, calls=%fused_computation.17 | convolution fusion | flops 3221225472 | bytes 11534336 | tf_op jit(solution)/shard_map/cond/branch_0_fun/dot_general | solution.py:96
  115.1 0.0 copy-done.4
  115.1 0.0 copy-done.5
  115.1 4.7 %multiply_convert_fusion.1 = bf16[1024,512]{1,0:T(8,128)(2,1)} fusion(f32[1024,512]{1,0:T(8,128)S(1)} %fusion.16, bf16[1024,3072]{1,0:T(8,128)(2,1)S(1)} %copy-done.4, bf16[1,3072,512]{2,1,0:T(8,128)(2,1)S(1)} %copy-done.5), kind=kOutput, calls=%fused_computation.21 | convolution fusion | flops 3224371200 | bytes 12582912 | tf_op jit(solution)/shard_map/cond/branch_0_fun/dot_general | solution.py:95
  119.8 0.0 copy-done
  119.8 6.5 %convolution_convert_fusion = bf16[1024,3072]{1,0:T(8,128)(2,1)} fusion(bf16[1024,512]{1,0:T(8,128)(2,1)} %get-tuple-element.56, bf16[1,512,3072]{2,1,0:T(8,128)(2,1)S(1)} %copy-done), kind=kOutput, calls=%fused_computation.22 | convolution fusion | flops 3224371200 | bytes 10485760 | tf_op jit(solution)/shard_map/dot_general | solution.py:104
  126.4 0.0 all-reduce.2.cloned.1.call-update
  126.4 131.8 %all-reduce.2.cloned.1.call-done = bf16[1024,3072]{1,0:T(8,128)(2,1)} async-done(((bf16[1024,3072]{1,0:T(8,128)(2,1)}), bf16[1024,3072]{1,0:T(8,128)(2,1)}) %all-reduce.2.cloned.1.call-update) | async-done | bytes 6291472 | tf_op jit(solution)/shard_map/psum | solution.py:105
  258.2 1.0 fusion.24
  259.2 20.0 %all_to_all.11 = bf16[8,8,3072]{2,1,0:T(8,128)(2,1)S(1)} all-to-all(bf16[8,8,3072]{2,1,0:T(8,128)(2,1)S(1)} %fusion.24), channel_id=1, replica_groups=mesh['role'=2,'grp'=8,'tp'=16] {'grp'}, dimensions={0} | all-to-all | bytes 786432 | tf_op jit(solution)/shard_map/all_to_all | solution.py:108
  279.3 4.8 %collective-permute-start.1 = (bf16[8,8,3072]{2,1,0:T(8,128)(2,1)S(1)}, bf16[8,8,3072]{2,1,0:T(8,128)(2,1)}, u32[]{:S(2)}, u32[]{:S(2)}) collective-permute-start(bf16[8,8,3072]{2,1,0:T(8,128)(2,1)S(1)} %all_to_all.11), channel_id=1, source_target_pairs={{128,0},{129,1},{130,2},{131,3},{132,4},{133,5},{134,6},{135,7},{1... | collective-permute-start | bytes 1179656 | tf_op jit(solution)/shard_map/ppermute | solution.py:18
  284.0 0.0 copy-done.2
  284.0 0.0 copy-done.3
  284.0 0.7 collective-permute-done.1
  284.7 1.8 fusion.23
  (7 shorter events, 0.1 us)
Async XLA Ops:
  6.5 113.3 %copy-start = (bf16[1,512,3072]{2,1,0:T(8,128)(2,1)S(1)}, bf16[1,512,3072]{2,1,0:T(8,128)(2,1)}, u32[]{:S(2)}) copy-start(bf16[1,512,3072]{2,1,0:T(8,128)(2,1)} %param.23) | copy-start | bytes 9437188
  6.5 101.9 %all-gather.2.cloned.1.call-start = ((), (), s32[]{:S(2)}) async-start(), calls=%async_computation.2 | async-start | bytes 6684672 | tf_op jit(solution)/shard_map/all_gather | solution.py:92
  9.4 14.8 %collective-permute-start = (bf16[8,8,3072]{2,1,0:T(8,128)(2,1)S(1)}, bf16[8,8,3072]{2,1,0:T(8,128)(2,1)S(1)}, u32[]{:S(2)}, u32[]{:S(2)}) collective-permute-start(bf16[8,8,3072]{2,1,0:T(8,128)(2,1)S(1)} %convolution_convert_fusion.1), channel_id=1, source_target_pairs={{0,128},{1,129},{2,130},{3,131},{4,132},{5,133},{6,134},{7,135},{8... | collective-permute-start | bytes 1179656 | tf_op jit(solution)/shard_map/ppermute | solution.py:18
  45.7 212.4 %all-reduce.2.cloned.1.call-start = ((), (), s32[]{:S(2)}) async-start(), calls=%async_computation.3 | async-start | bytes 12582912 | tf_op jit(solution)/shard_map/psum | solution.py:105
  108.5 6.6 %copy-start.4 = (bf16[1024,3072]{1,0:T(8,128)(2,1)S(1)}, bf16[1024,3072]{1,0:T(8,128)(2,1)}, u32[]{:S(2)}) copy-start(bf16[1024,3072]{1,0:T(8,128)(2,1)} %get-tuple-element.34) | copy-start | bytes 18874372 | tf_op jit(solution)/shard_map/cond
  108.5 6.6 %copy-start.5 = (bf16[1,3072,512]{2,1,0:T(8,128)(2,1)S(1)}, bf16[1,3072,512]{2,1,0:T(8,128)(2,1)}, u32[]{:S(2)}) copy-start(bf16[1,3072,512]{2,1,0:T(8,128)(2,1)} %get-tuple-element.49) | copy-start | bytes 9437188 | tf_op jit(solution)/shard_map/cond
  126.4 157.6 %copy-start.2 = (s32[16,2]{0,1:T(2,128)S(1)}, s32[16,2]{0,1:T(2,128)}, u32[]{:S(2)}) copy-start(s32[16,2]{0,1:T(2,128)} %param.19) | copy-start | bytes 388
  126.4 157.6 %copy-start.3 = (f32[16,2]{0,1:T(2,128)S(1)}, f32[16,2]{0,1:T(2,128)}, u32[]{:S(2)}) copy-start(f32[16,2]{0,1:T(2,128)} %param.20) | copy-start | bytes 388
  279.3 5.5 %collective-permute-start.1 = (bf16[8,8,3072]{2,1,0:T(8,128)(2,1)S(1)}, bf16[8,8,3072]{2,1,0:T(8,128)(2,1)}, u32[]{:S(2)}, u32[]{:S(2)}) collective-permute-start(bf16[8,8,3072]{2,1,0:T(8,128)(2,1)S(1)} %all_to_all.11), channel_id=1, source_target_pairs={{128,0},{129,1},{130,2},{131,3},{132,4},{133,5},{134,6},{135,7},{1... | collective-permute-start | bytes 1179656 | tf_op jit(solution)/shard_map/ppermute | solution.py:18
Sparse Core Ops, SparseCore 0:
  45.9 62.5 all-gather.1
  126.5 131.6 all-reduce.1
where the time goes:
time: 294 us; the launch traced here: 293 us
  waiting for transfers between devices  209 us (71%)
  blocking collectives  41.5 us (14%)
  matrix products  20.8 us (7%)
  between operations  13.4 us (5%)
  starting transfers between devices  6.1 us (2%)
    psum x1, waiting for transfers between devices, local(): lax.psum(partial_sums.astype(jnp.bfloat16), 'tp').astype(jnp.float32)  132 us
    all_gather x1, waiting for transfers between devices, local(): shard_rows = lax.all_gather(tok_rows, 'tp', axis=0, tiled=True)  62.7 us
    all_to_all x1, blocking collectives, local(): lax.all_to_all(arrived, 'grp', split_axis=0, concat_axis=0, tiled=True)  21.4 us
    all_to_all x1, blocking collectives, local(): lax.all_to_all(expert_out, 'grp', split_axis=0, concat_axis=0, tiled=True)  20 us
    ppermute x2, waiting for transfers between devices, shifted(): return lax.ppermute(x, axis, pairs)  14.3 us
    dot_general x1, matrix products, compute(): up_part = jnp.dot(shard_rows, up_weight, preferred_element_type=jnp.float32)  6.58 us
    dot_general x1, matrix products, local(): jnp.dot(hidden, down_weight, preferred_element_type=jnp.float32)  6.54 us
    ppermute x2, starting transfers between devices, shifted(): return lax.ppermute(x, axis, pairs)  6.05 us
  transfers between devices with their start and end apart: 4, of which 4 were waited for; matrix products, arithmetic and copies ran while one was open for 0% of the time, Pallas kernels for 0%

commit v1 on v0

v1 whole, which is shorter than its diff:
```python
import functools
import math

import jax
import jax.numpy as jnp
from jax import lax
from jax.experimental import pallas as pl
from jax.experimental.pallas import tpu as pltpu
from jax.sharding import PartitionSpec as P

HEAD_WIDTH = 128
QUERY_HEADS = 24
KEY_VALUE_HEADS = 4
MODEL_WIDTH = 3072
REQUESTS = 16
POSITIONS = 128
WIDE = 512
QUARTER = 768
HALF = 1536
EIGHTH = 384
ROWS = 16
OFFSETS = (0, 1, -1, 2, -2, 3, -3, 4)
MESH = pl.DeviceIdType.MESH
F32 = jnp.float32
BF16 = jnp.bfloat16


def iota(shape, axis):
    return lax.broadcasted_iota(jnp.int32, shape, axis)


def one_hot(mask):
    return jnp.where(mask, 1.0, 0.0).astype(BF16)


def dot(a, b):
    return jnp.dot(a, b, preferred_element_type=F32)


def offset_of(index):
    step = (index + 1) // 2
    return jnp.where(index % 2 == 1, step, -step)


def kernel(
    q_ref, k_hbm, v_hbm, len_ref, gain_ref, ids_ref, gates_ref, wg_hbm, wu_hbm, wd_hbm,
    out_ref,
    k_buf, v_buf, wg, wu, wd, q_rows, s_rows, c_rows,
    packed, landed, xs, hidden, parts, r1, r2, r3, r4, r5, r6, back, home,
    kv_sem, w_sem, z_send, z_recv, ag_send, ag_recv, rs_send, rs_recv, ret_send, ret_recv,
):
    role = lax.axis_index("role")
    z = lax.axis_index("grp")
    t = lax.axis_index("tp")
    x, y = t % 4, t // 4
    turn = 1 - 2 * role

    def at_x(step):
        return (role, z, y * 4 + (x + step * turn + 4) % 4)

    def at_y(step):
        return (role, z, ((y + step * turn + 4) % 4) * 4 + x)

    def at_z(step, core):
        return (core, (z + step + 8) % 8, t)

    near = {"x": at_x, "y": at_y}

    loads = []
    for i in range(4):
        rows = pl.ds(4 * i, 4)
        loads.append((
            pltpu.make_async_copy(k_hbm.at[rows], k_buf.at[rows], kv_sem.at[i]),
            pltpu.make_async_copy(v_hbm.at[rows], v_buf.at[rows], kv_sem.at[4 + i]),
        ))
    for kc, _ in loads:
        kc.start()
    for _, vc in loads:
        vc.start()
    weight_loads = [
        pltpu.make_async_copy(src.at[0], dst, w_sem.at[i])
        for i, (src, dst) in enumerate(((wg_hbm, wg), (wu_hbm, wu), (wd_hbm, wd)))
    ]
    for wc in weight_loads:
        wc.start()

    barrier = pltpu.get_barrier_semaphore()
    partners = [at_x(1), at_x(-1), at_y(1), at_y(-1), at_z(0, 1 - role)]
    for step in OFFSETS[1:]:
        partners += [at_z(step, role), at_z(step, 1 - role)]
    for partner in partners:
        pl.semaphore_signal(barrier, inc=1, device_id=partner, device_id_type=MESH)

    for h in range(QUERY_HEADS):
        q_rows[pl.ds(h, REQUESTS, stride=QUERY_HEADS), :] = q_ref[
            :, h * HEAD_WIDTH : (h + 1) * HEAD_WIDTH
        ].astype(F32)
    group = iota((QUERY_HEADS, HEAD_WIDTH), 0) // (QUERY_HEADS // KEY_VALUE_HEADS)
    place = iota((QUERY_HEADS, POSITIONS), 1)
    scale = 1.0 / math.sqrt(HEAD_WIDTH)
    for r in range(REQUESTS):
        if r % 4 == 0:
            loads[r // 4][0].wait()
        own = q_rows[r * QUERY_HEADS : (r + 1) * QUERY_HEADS, :]
        spread = jnp.concatenate(
            [jnp.where(group == j, own, 0.0) for j in range(KEY_VALUE_HEADS)], axis=1
        ).astype(BF16)
        scores = lax.dot_general(
            spread, k_buf[r], (((1,), (1,)), ((), ())), preferred_element_type=F32
        )
        s_rows[r * QUERY_HEADS : (r + 1) * QUERY_HEADS, :] = jnp.where(
            place < len_ref[r], scores * scale, -jnp.inf
        )
    scores = s_rows[...]
    raised = jnp.exp(scores - jnp.max(scores, axis=1, keepdims=True))
    s_rows[...] = raised / jnp.sum(raised, axis=1, keepdims=True)
    for r in range(REQUESTS):
        if r % 4 == 0:
            loads[r // 4][1].wait()
        weights = s_rows[r * QUERY_HEADS : (r + 1) * QUERY_HEADS, :].astype(BF16)
        mixed = dot(weights, v_buf[r])
        own = jnp.where(group == 0, mixed[:, :HEAD_WIDTH], 0.0)
        for j in range(1, KEY_VALUE_HEADS):
            own = jnp.where(group == j, mixed[:, j * HEAD_WIDTH : (j + 1) * HEAD_WIDTH], own)
        c_rows[r * QUERY_HEADS : (r + 1) * QUERY_HEADS, :] = own
    heads = [
        c_rows[pl.ds(h, REQUESTS, stride=QUERY_HEADS), :] for h in range(QUERY_HEADS)
    ]
    squares = heads[0] * heads[0]
    for head in heads[1:]:
        squares = squares + head * head
    mean_square = jnp.sum(squares, axis=1, keepdims=True) / MODEL_WIDTH
    norm = lax.rsqrt(mean_square + 1e-05)
    expert_in = [
        head * norm * gain_ref[:, h * HEAD_WIDTH : (h + 1) * HEAD_WIDTH]
        for h, head in enumerate(heads)
    ]
    stacked = jnp.concatenate(
        [jnp.concatenate(expert_in[6 * i : 6 * i + 6], axis=1) for i in range(4)], axis=0
    ).astype(BF16)

    diagonal = iota((16, 16), 0) == iota((16, 16), 1)
    first = jnp.sum(jnp.where(diagonal, ids_ref[:, 0:1], 0), axis=0, keepdims=True)
    second = jnp.sum(jnp.where(diagonal, ids_ref[:, 1:2], 0), axis=0, keepdims=True)
    first = jnp.concatenate([first] * 4, axis=1)
    second = jnp.concatenate([second] * 4, axis=1)
    row, col = iota((128, 64), 0), iota((128, 64), 1)
    expert = (z + offset_of(row // 16) + 8) % 8
    hit = (first == expert) | (second == expert)
    trow, tcol = iota((64, 64), 0), iota((64, 64), 1)
    earlier = (trow // 16 == tcol // 16) & (trow % 16 < tcol % 16)
    rank = dot(one_hot(hit), one_hot(earlier))
    slot = ((row // 4) % 4 + 4 * role).astype(F32)
    chosen = one_hot(hit & (rank == slot) & (row % 4 == col // 16))
    packets = dot(chosen, stacked).astype(BF16)
    packed[...] = packets.reshape(8, ROWS, QUARTER)

    pl.semaphore_wait(barrier, len(partners))

    z_copies = {}
    for j in range(1, 8):
        z_copies[j] = pltpu.make_async_remote_copy(
            src_ref=packed.at[j], dst_ref=landed.at[j],
            send_sem=z_send.at[j], recv_sem=z_recv.at[j],
            device_id=at_z(OFFSETS[j], role), device_id_type=MESH,
        )
        z_copies[j].start()
    landed[0] = packets[:ROWS]

    def spot(part, u, v):
        return v, 4 * part + u

    def chunk(ref, part, u, v):
        block, place = spot(part, u, v)
        return ref.at[block, pl.ds(place * ROWS, ROWS), :]

    axes = (("x", "y"), ("y", "x"))
    gathers = {}

    def send_chunk(part, axis, step, src, dst):
        number = part * 16 + dst[0] * 4 + dst[1]
        copy = pltpu.make_async_remote_copy(
            src_ref=chunk(xs, part, *src), dst_ref=chunk(xs, part, *dst),
            send_sem=ag_send.at[number], recv_sem=ag_recv.at[number],
            device_id=near[axes[part][axis]](step), device_id_type=MESH,
        )
        copy.start()
        gathers[part, dst[0], dst[1]] = copy

    pick_row, pick_col = iota((ROWS, 64), 0), iota((ROWS, 64), 1)
    for part in range(2):
        for j in range(4 * part, 4 * part + 4):
            if j > 0:
                z_copies[j].wait_recv()
        rows = landed[4 * part : 4 * part + 4].reshape(64, QUARTER)
        for i in range(4):
            pick = one_hot((pick_col // 4 == pick_row) & (pick_col % 4 == i))
            xs[0, 64 * part : 64 * part + ROWS, i * QUARTER : (i + 1) * QUARTER] = dot(
                pick, rows
            ).astype(BF16)
        send_chunk(part, 0, 1, (0, 0), (1, 0))
        send_chunk(part, 0, -1, (0, 0), (3, 0))
        send_chunk(part, 1, 1, (0, 0), (0, 1))
        send_chunk(part, 1, -1, (0, 0), (0, 3))

    for part in range(2):
        gathers[part, 1, 0].wait_recv()
        send_chunk(part, 0, 1, (1, 0), (2, 0))
        send_chunk(part, 1, 1, (1, 0), (1, 1))
        send_chunk(part, 1, -1, (1, 0), (1, 3))
    for part in range(2):
        gathers[part, 3, 0].wait_recv()
        send_chunk(part, 1, 1, (3, 0), (3, 1))
        send_chunk(part, 1, -1, (3, 0), (3, 3))
    for part in range(2):
        gathers[part, 0, 1].wait_recv()
        send_chunk(part, 1, 1, (0, 1), (0, 2))
    for part in range(2):
        gathers[part, 2, 0].wait_recv()
        send_chunk(part, 1, 1, (2, 0), (2, 1))
        send_chunk(part, 1, -1, (2, 0), (2, 3))

    def pass_on(u):
        for part in range(2):
            gathers[part, u, 1].wait_recv()
            send_chunk(part, 1, 1, (u, 1), (u, 2))

    def gate_up(block, i):
        cols = slice(i * 256, (i + 1) * 256)
        rows = xs[block]
        gate = dot(rows, wg[:, cols])
        up = dot(rows, wu[:, cols])
        hidden[:, cols] = (gate / (1.0 + jnp.exp(-gate)) * up).astype(BF16)

    def down(block, low, high):
        for i in range(low, high):
            cols = slice(i * 512, (i + 1) * 512)
            parts[block, :, cols] = dot(hidden[...], wd[:, cols]).astype(BF16)

    for wc in weight_loads:
        wc.wait()
    gate_up(0, 0)
    pass_on(1)
    gate_up(0, 1)
    pass_on(3)
    down(0, 0, 6)
    pass_on(2)

    def ready(v):
        for part in range(2):
            for u in range(4):
                gathers[part, u, v].wait_recv()

    sums = {}

    def send_sum(buf, base, part, u, axis, step, src):
        number = base + (part * 4 + u if base < 24 else part)
        dst = buf.at[part, u] if base < 24 else buf.at[part]
        copy = pltpu.make_async_remote_copy(
            src_ref=src, dst_ref=dst,
            send_sem=rs_send.at[number], recv_sem=rs_recv.at[number],
            device_id=near[axes[part][axis]](step), device_id_type=MESH,
        )
        copy.start()
        sums[base, part, u] = copy

    order = (2, 1, 3, 0)
    for part in range(2):
        for u in range(4):
            gathers[part, u, 3].wait_recv()
    gate_up(3, 0)
    gate_up(3, 1)
    down(3, 0, 6)
    for u in order:
        for part in range(2):
            send_sum(r2, 0, part, u, 1, 1, chunk(parts, part, u, 3))
    gate_up(1, 0)
    gate_up(1, 1)
    down(1, 0, 6)
    ready(2)
    gate_up(2, 0)
    gate_up(2, 1)
    down(2, 0, 6)
    for u in order:
        for part in range(2):
            send_sum(r1, 8, part, u, 1, -1, chunk(parts, part, u, 2))
    for u in order:
        for part in range(2):
            sums[8, part, u].wait_recv()
            mine = chunk(parts, part, u, 1)
            mine[...] = (mine[...].astype(F32) + r1[part, u].astype(F32)).astype(BF16)
            send_sum(r3, 16, part, u, 1, -1, mine)
    for u in order:
        for part in range(2):
            sums[0, part, u].wait_recv()
            sums[16, part, u].wait_recv()
            mine = chunk(parts, part, u, 0)
            mine[...] = (
                mine[...].astype(F32) + r2[part, u].astype(F32) + r3[part, u].astype(F32)
            ).astype(BF16)
            if u == 2:
                send_sum(r4, 24, part, u, 0, -1, mine)
            if u == 3:
                send_sum(r5, 26, part, u, 0, 1, mine)
    for part in range(2):
        sums[24, part, 2].wait_recv()
        mine = chunk(parts, part, 1, 0)
        mine[...] = (mine[...].astype(F32) + r4[part].astype(F32)).astype(BF16)
        send_sum(r6, 28, part, 1, 0, -1, mine)

    returns = []
    spread_row, spread_col = iota((64, ROWS), 0), iota((64, ROWS), 1)
    for part in range(2):
        sums[26, part, 3].wait_recv()
        sums[28, part, 1].wait_recv()
        total = (
            chunk(parts, part, 0, 0)[...].astype(F32)
            + r5[part].astype(F32)
            + r6[part].astype(F32)
        ).astype(BF16)
        for half in range(2):
            rows = None
            for i in range(4):
                pick = one_hot((spread_row // 4 == spread_col) & (spread_row % 4 == i))
                low = half * HALF + i * EIGHTH
                term = dot(pick, total[:, low : low + EIGHTH])
                rows = term if rows is None else rows + term
            back[half, 4 * part : 4 * part + 4] = rows.astype(BF16).reshape(4, ROWS, EIGHTH)
        for j in range(4 * part, 4 * part + 4):
            for other in range(2):
                half = role if other == 0 else 1 - role
                if j == 0 and other == 0:
                    continue
                number = j * 2 + other
                copy = pltpu.make_async_remote_copy(
                    src_ref=back.at[half, j], dst_ref=home.at[j, role],
                    send_sem=ret_send.at[number], recv_sem=ret_recv.at[number],
                    device_id=at_z(-OFFSETS[j], half), device_id_type=MESH,
                )
                copy.start()
                returns.append(copy)
        if part == 0:
            home[0, role] = back[role, 0]

    row, col = iota((REQUESTS, 256), 0), iota((REQUESTS, 256), 1)
    expert = (z + offset_of(col // 32) + 8) % 8
    hits = [ids_ref[:, k : k + 1] == expert for k in range(2)]
    earlier = one_hot(iota((16, 16), 1) < iota((16, 16), 0))
    rank = dot(earlier, one_hot(hits[0] | hits[1]))
    fits = rank == ((col // 4) % 8).astype(F32)
    for copy in returns:
        copy.wait_recv()
    rows = home[...].reshape(256, EIGHTH)
    for i in range(4):
        terms = [
            dot(one_hot(hits[k] & fits & (col % 4 == i)), rows) * gates_ref[:, k : k + 1]
            for k in range(2)
        ]
        out_ref[:, i * EIGHTH : (i + 1) * EIGHTH] = (terms[0] + terms[1]).astype(BF16)

    for copy in z_copies.values():
        copy.wait_send()
    for copy in gathers.values():
        copy.wait_send()
    for copy in sums.values():
        copy.wait_send()
    for copy in returns:
        copy.wait_send()


def local(
    queries, cached_keys, cached_values, lengths, norm_gain,
    expert_ids, gates, gate_proj, up_proj, down_proj,
):
    vmem = pl.BlockSpec(memory_space=pltpu.VMEM)
    smem = pl.BlockSpec(memory_space=pltpu.SMEM)
    hbm = pl.BlockSpec(memory_space=pl.ANY)
    dma = pltpu.SemaphoreType.DMA
    return pl.pallas_call(
        kernel,
        out_shape=jax.ShapeDtypeStruct((REQUESTS, HALF), BF16),
        in_specs=[vmem, hbm, hbm, smem, vmem, vmem, vmem, hbm, hbm, hbm],
        out_specs=vmem,
        scratch_shapes=[
            pltpu.VMEM((REQUESTS, POSITIONS, WIDE), BF16),
            pltpu.VMEM((REQUESTS, POSITIONS, WIDE), BF16),
            pltpu.VMEM((MODEL_WIDTH, WIDE), BF16),
            pltpu.VMEM((MODEL_WIDTH, WIDE), BF16),
            pltpu.VMEM((WIDE, MODEL_WIDTH), BF16),
            pltpu.VMEM((REQUESTS * QUERY_HEADS, HEAD_WIDTH), F32),
            pltpu.VMEM((REQUESTS * QUERY_HEADS, HEAD_WIDTH), F32),
            pltpu.VMEM((REQUESTS * QUERY_HEADS, HEAD_WIDTH), F32),
            pltpu.VMEM((8, ROWS, QUARTER), BF16),
            pltpu.VMEM((8, ROWS, QUARTER), BF16),
            pltpu.VMEM((4, 128, MODEL_WIDTH), BF16),
            pltpu.VMEM((128, WIDE), BF16),
            pltpu.VMEM((4, 128, MODEL_WIDTH), BF16),
            pltpu.VMEM((2, 4, ROWS, MODEL_WIDTH), BF16),
            pltpu.VMEM((2, 4, ROWS, MODEL_WIDTH), BF16),
            pltpu.VMEM((2, 4, ROWS, MODEL_WIDTH), BF16),
            pltpu.VMEM((2, ROWS, MODEL_WIDTH), BF16),
            pltpu.VMEM((2, ROWS, MODEL_WIDTH), BF16),
            pltpu.VMEM((2, ROWS, MODEL_WIDTH), BF16),
            pltpu.VMEM((2, 8, ROWS, EIGHTH), BF16),
            pltpu.VMEM((8, 2, ROWS, EIGHTH), BF16),
            dma((8,)), dma((3,)), dma((8,)), dma((8,)), dma((32,)), dma((32,)),
            dma((30,)), dma((30,)), dma((16,)), dma((16,)),
        ],
        compiler_params=pltpu.CompilerParams(
            collective_id=0, has_side_effects=True, vmem_limit_bytes=56 * 1024 * 1024
        ),
        cost_estimate=pl.CostEstimate(
            flops=5_000_000_000, bytes_accessed=14_000_000, transcendentals=400_000
        ),
    )(
        queries, cached_keys, cached_values, lengths, norm_gain.reshape(1, MODEL_WIDTH),
        expert_ids, gates, gate_proj, up_proj, down_proj,
    )


def solution(mesh):
    placed = (
        P(("grp", "tp"), None),
        P(("grp", "tp"), None, None),
        P(("grp", "tp"), None, None),
        P(("grp", "tp")),
        P(),
        P(("grp", "tp"), None),
        P(("grp", "tp"), None),
        P("grp", None, "tp"),
        P("grp", None, "tp"),
        P("grp", "tp", None),
    )
    return jax.shard_map(
        local, mesh=mesh, in_specs=placed, out_specs=P(("grp", "tp"), "role"), check_vma=False
    )
```

time: 294 us -> 69.7 us (0.24)
  waiting for transfers between devices: 209 us -> 0 us
  Pallas kernels: 0 us -> 65.4 us
  blocking collectives: 41.5 us -> 0 us
  matrix products: 20.8 us -> 0 us
  between operations: 13.4 us -> 0.01 us
  starting transfers between devices: 6.1 us -> 0 us
  local copies, waits for them, and re-layouts: 0.9 us -> 4.12 us
    psum x1 -> x0, waiting for transfers between devices: 132 us -> none  [local(): lax.psum(partial_sums.astype(jnp.bfloat16), 'tp').astype(jnp.float32)]
    pallas_call x0 -> x1, Pallas kernels: none -> 65.4 us  [local(): pl.pallas_call(kernel, out_shape=jax.ShapeDtypeStruct((REQUESTS, HALF), B...]
    all_gather x1 -> x0, waiting for transfers between devices: 62.7 us -> none  [local(): shard_rows = lax.all_gather(tok_rows, 'tp', axis=0, tiled=True)]
    all_to_all x2 -> x0, blocking collectives: 41.5 us -> none  [the longest x1 21.4 us: local(): lax.all_to_all(arrived, 'grp', split_axis=0, concat_axis=0, tiled=True)]
    dot_general x5 -> x0, matrix products: 20.8 us -> none  [the longest x1 6.58 us: compute(): up_part = jnp.dot(shard_rows, up_weight, preferred_element_type=jnp.float32)]
    ppermute x2 -> x0, waiting for transfers between devices: 14.3 us -> none  [shifted(): return lax.ppermute(x, axis, pairs)]
    ppermute x2 -> x0, starting transfers between devices: 6.05 us -> none  [shifted(): return lax.ppermute(x, axis, pairs)]
    unnamed x6 -> x3, local copies, waits for them, and re-layouts: 0.01 us -> 4.12 us
  transfers between devices with their start and end apart: 4 -> 0, of which waited for: 4 -> 0; matrix products, arithmetic and copies ran while one was open for 0% -> 0% of each run, Pallas kernels for 0% -> 0%
where the time goes in v1:
time: 69.7 us; the launch traced here: 69.5 us
  Pallas kernels  65.4 us (94%)
  local copies, waits for them, and re-layouts  4.12 us (6%)
    pallas_call x1, Pallas kernels, local(): pl.pallas_call(kernel, out_shape=jax.ShapeDtypeStruct((REQUESTS, HALF), B...  65.4 us
    unnamed x3, local copies, waits for them, and re-layouts  4.12 us

profile of v1, /device:TPU:1, one launch (start us, length us, event | category | flops | bytes accessed | tf_op | source)
XLA Modules:
  0.0 69.5 jit_solution(16212371268049900684)
XLA Ops:
  0.0 1.4 %copy.11.ids_ref = s32[16,2]{1,0:T(8,128)} copy(s32[16,2]{0,1:T(2,128)} %param.15) | data formatting | bytes 256 | tf_op args[5]
  1.4 1.3 %copy.12.gates_ref = f32[16,2]{1,0:T(8,128)} copy(f32[16,2]{0,1:T(2,128)} %param.16) | data formatting | bytes 256 | tf_op args[6]
  2.7 65.4 %shard_map.100 = bf16[16,1536]{1,0:T(8,128)(2,1)} custom-call(bf16[16,3072]{1,0:T(8,128)(2,1)} %q_ref.1, bf16[16,128,512]{2,1,0:T(8,128)(2,1)} %k_hbm.1, bf16[16,128,512]{2,1,0:T(8,128)(2,1)} %v_hbm.1, s32[16]{0:T(128)} %len_ref.1, f32[1,3072]{1,0:T(1,128)} %bitcast.1, s32[16,2]{1,0:T(8,128)} %copy.11.ids_ref, f32[16,2]{1,0:T(8,128)} %copy.12.gates_ref, ...), custom_call_target="tpu_custom_call" | custom-call | flops 5000000000 | bytes 14000000 | tf_op jit(solution)/shard_map/pallas_call | solution.py:379
  68.1 1.4 %copy.14 = bf16[16,1536]{1,0:T(8,128)(2,1)} copy(bf16[16,1536]{1,0:T(8,128)(2,1)} %shard_map.100) | data formatting | bytes 98304

commit v2 on v1

v2 whole, which is shorter than its diff:
```python
import functools
import math

import jax
import jax.numpy as jnp
from jax import lax
from jax.experimental import pallas as pl
from jax.experimental.pallas import tpu as pltpu
from jax.sharding import PartitionSpec as P

HEAD_WIDTH = 128
QUERY_HEADS = 24
KEY_VALUE_HEADS = 4
MODEL_WIDTH = 3072
REQUESTS = 16
POSITIONS = 128
WIDE = 512
QUARTER = 768
HALF = 1536
EIGHTH = 384
ROWS = 16
OFFSETS = (0, 1, -1, 2, -2, 3, -3, 4)
PIECES = 1
MIX = (1, 0)
SPAN = 3072
FIRST_BLOCK = 0
ORDER = (
    ("unpack", 0), ("own", 0, 0, 0, 1), ("own", 0, 0, 0, -1), ("own", 0, 0, 1, 1),
    ("own", 0, 0, 1, -1), ("far", 0, 0), ("unpack", 1), ("own", 1, 0, 0, 1), ("own", 1, 0, 0, -1),
    ("own", 1, 0, 1, 1), ("own", 1, 0, 1, -1), ("far", 1, 0), ("across", 0, 0, 1, 1),
    ("across", 0, 0, 1, -1), ("across", 1, 0, 1, 1), ("across", 1, 0, 1, -1),
    ("across", 0, 0, 3, 1), ("across", 0, 0, 3, -1), ("across", 1, 0, 3, 1),
    ("across", 1, 0, 3, -1), ("pass", 0, 0, 0), ("pass", 1, 0, 0), ("across", 0, 0, 2, 1),
    ("across", 0, 0, 2, -1), ("across", 1, 0, 2, 1), ("across", 1, 0, 2, -1), ("experts", 0, 0),
    ("pass", 0, 0, 1), ("pass", 1, 0, 1), ("pass", 0, 0, 3), ("pass", 1, 0, 3), ("pass", 0, 0, 2),
    ("pass", 1, 0, 2), ("experts", 0, 3), ("direct", 1, 0, 2), ("direct", 0, 0, 2),
    ("direct", 1, 0, 1), ("direct", 0, 0, 1), ("direct", 1, 0, 3), ("direct", 0, 0, 3),
    ("direct", 1, 0, 0), ("direct", 0, 0, 0), ("experts", 0, 1), ("experts", 0, 2),
    ("opposite", 1, 0, 2), ("opposite", 0, 0, 2), ("opposite", 1, 0, 1), ("opposite", 0, 0, 1),
    ("opposite", 1, 0, 3), ("opposite", 0, 0, 3), ("opposite", 1, 0, 0), ("opposite", 0, 0, 0),
    ("sum", 1, 0, 2), ("sum", 0, 0, 2), ("sum", 1, 0, 1), ("sum", 0, 0, 1), ("sum", 1, 0, 3),
    ("sum", 0, 0, 3), ("sum", 1, 0, 0), ("sum", 0, 0, 0), ("line", 1, 0, 2), ("line", 0, 0, 2),
    ("line", 1, 0, 1), ("line", 0, 0, 1), ("line", 1, 0, 3), ("line", 0, 0, 3), ("line", 1, 0, 0),
    ("line", 0, 0, 0), ("give", 1, 0), ("give", 0, 0),
)
MESH = pl.DeviceIdType.MESH
F32 = jnp.float32
BF16 = jnp.bfloat16


def iota(shape, axis):
    return lax.broadcasted_iota(jnp.int32, shape, axis)


def one_hot(mask):
    return jnp.where(mask, 1.0, 0.0).astype(BF16)


def dot(a, b):
    return jnp.dot(a, b, preferred_element_type=F32)


def offset_of(index):
    step = (index + 1) // 2
    return jnp.where(index % 2 == 1, step, -step)


def kernel(
    q_hbm, k_hbm, v_hbm, len_ref, gain_hbm, ids_hbm, gates_hbm, wg_hbm, wu_hbm, wd_hbm,
    out_ref,
    q_buf, gain, ids, gates, k_buf, v_buf, wg, wu, wd, q_rows, s_rows, c_rows,
    packed, landed, xs, hidden, parts, r1, r2, r3, r4, r5, r6, back, home, table,
    small_sem, kv_sem, w_sem, z_send, z_recv, ag_send, ag_recv, rs_send, rs_recv,
    ret_send, ret_recv,
):
    role = lax.axis_index("role")
    z = lax.axis_index("grp")
    t = lax.axis_index("tp")
    x, y = t % 4, t // 4
    turn = 1 - 2 * role

    def at(w, axis, step):
        along_x = int(axis == w)
        col = (x + step * turn * along_x + 4) % 4
        row = (y + step * turn * (1 - along_x) + 4) % 4
        return (role, z, row * 4 + col)

    def at_z(step, core):
        return (core, (z + step + 8) % 8, t)

    barrier = pltpu.get_barrier_semaphore()
    partners = [at(0, a, step) for a in (0, 1) for step in (1, -1, 2)] + [at_z(0, 1 - role)]
    for step in OFFSETS[1:]:
        partners += [at_z(step, role), at_z(step, 1 - role)]
    for partner in partners:
        pl.semaphore_signal(barrier, inc=1, device_id=partner, device_id_type=MESH)

    small = [
        pltpu.make_async_copy(src, dst, small_sem.at[i])
        for i, (src, dst) in enumerate(
            ((q_hbm, q_buf), (ids_hbm, ids), (gain_hbm, gain), (gates_hbm, gates))
        )
    ]
    loads = []
    for i in range(4):
        rows = pl.ds(4 * i, 4)
        loads.append((
            pltpu.make_async_copy(k_hbm.at[rows], k_buf.at[rows], kv_sem.at[i]),
            pltpu.make_async_copy(v_hbm.at[rows], v_buf.at[rows], kv_sem.at[4 + i]),
        ))
    weight_loads = [
        pltpu.make_async_copy(src.at[0], dst, w_sem.at[i])
        for i, (src, dst) in enumerate(((wg_hbm, wg), (wu_hbm, wu), (wd_hbm, wd)))
    ]
    small[0].start()
    for kc, _ in loads:
        kc.start()
    for _, vc in loads:
        vc.start()
    for copy in small[1:]:
        copy.start()

    small[0].wait()
    for h in range(QUERY_HEADS):
        q_rows[pl.ds(h, REQUESTS, stride=QUERY_HEADS), :] = q_buf[
            :, h * HEAD_WIDTH : (h + 1) * HEAD_WIDTH
        ].astype(F32)
    group = iota((QUERY_HEADS, HEAD_WIDTH), 0) // (QUERY_HEADS // KEY_VALUE_HEADS)
    place = iota((QUERY_HEADS, POSITIONS), 1)
    scale = 1.0 / math.sqrt(HEAD_WIDTH)
    for r in range(REQUESTS):
        if r % 4 == 0:
            loads[r // 4][0].wait()
        own = q_rows[r * QUERY_HEADS : (r + 1) * QUERY_HEADS, :]
        spread = jnp.concatenate(
            [jnp.where(group == j, own, 0.0) for j in range(KEY_VALUE_HEADS)], axis=1
        ).astype(BF16)
        scores = lax.dot_general(
            spread, k_buf[r], (((1,), (1,)), ((), ())), preferred_element_type=F32
        )
        s_rows[r * QUERY_HEADS : (r + 1) * QUERY_HEADS, :] = jnp.where(
            place < len_ref[r], scores * scale, -jnp.inf
        )
    for wc in weight_loads:
        wc.start()
    scores = s_rows[...]
    raised = jnp.exp(scores - jnp.max(scores, axis=1, keepdims=True))
    s_rows[...] = raised / jnp.sum(raised, axis=1, keepdims=True)
    for r in range(REQUESTS):
        if r % 4 == 0:
            loads[r // 4][1].wait()
        weights = s_rows[r * QUERY_HEADS : (r + 1) * QUERY_HEADS, :].astype(BF16)
        mixed = dot(weights, v_buf[r])
        own = jnp.where(group == 0, mixed[:, :HEAD_WIDTH], 0.0)
        for j in range(1, KEY_VALUE_HEADS):
            own = jnp.where(group == j, mixed[:, j * HEAD_WIDTH : (j + 1) * HEAD_WIDTH], own)
        c_rows[r * QUERY_HEADS : (r + 1) * QUERY_HEADS, :] = own
    for copy in small[1:]:
        copy.wait()
    heads = [
        c_rows[pl.ds(h, REQUESTS, stride=QUERY_HEADS), :] for h in range(QUERY_HEADS)
    ]
    squares = heads[0] * heads[0]
    for head in heads[1:]:
        squares = squares + head * head
    mean_square = jnp.sum(squares, axis=1, keepdims=True) / MODEL_WIDTH
    norm = lax.rsqrt(mean_square + 1e-05)
    expert_in = [
        head * norm * gain[:, h * HEAD_WIDTH : (h + 1) * HEAD_WIDTH]
        for h, head in enumerate(heads)
    ]
    stacked = jnp.concatenate(
        [jnp.concatenate(expert_in[6 * i : 6 * i + 6], axis=1) for i in range(4)], axis=0
    ).astype(BF16)

    diagonal = iota((16, 16), 0) == iota((16, 16), 1)
    first = jnp.concatenate([ids[0:1, :]] * 4, axis=1)
    second = jnp.concatenate([ids[1:2, :]] * 4, axis=1)
    row, col = iota((128, 64), 0), iota((128, 64), 1)
    expert = (z + turn * offset_of(row // 16) + 8) % 8
    hit = (first == expert) | (second == expert)
    trow, tcol = iota((64, 64), 0), iota((64, 64), 1)
    earlier = (trow // 16 == tcol // 16) & (trow % 16 < tcol % 16)
    rank = dot(one_hot(hit), one_hot(earlier))
    slot = ((row // 4) % 4 + 4 * role).astype(F32)
    chosen = one_hot(hit & (rank == slot) & (row % 4 == col // 16))
    packets = dot(chosen, stacked).astype(BF16)
    packed[...] = packets.reshape(8, ROWS, QUARTER)

    pl.semaphore_wait(barrier, len(partners))

    z_copies = {}
    for j in range(1, 8):
        z_copies[j] = pltpu.make_async_remote_copy(
            src_ref=packed.at[j], dst_ref=landed.at[j],
            send_sem=z_send.at[j], recv_sem=z_recv.at[j],
            device_id=at_z(turn * OFFSETS[j], role), device_id_type=MESH,
        )
        z_copies[j].start()
    landed[0] = packets[:ROWS]

    def piece(ref, w, h, u, v):
        rows = pl.ds((w * 4 + u) * ROWS, ROWS)
        return ref.at[v, rows, pl.ds(h * SPAN, SPAN)]

    copies = {}
    seen = set()

    def arrived(key):
        if key not in seen:
            seen.add(key)
            copies[key].wait_recv()

    def gather(w, h, axis, step, u, v):
        du, dv = ((u + step) % 4, v) if axis == 0 else (u, (v + step) % 4)
        number = ((w * PIECES + h) * 4 + du) * 4 + dv
        copy = pltpu.make_async_remote_copy(
            src_ref=piece(xs, w, h, u, v), dst_ref=piece(xs, w, h, du, dv),
            send_sem=ag_send.at[number], recv_sem=ag_recv.at[number],
            device_id=at(w, axis, step), device_id_type=MESH,
        )
        copy.start()
        copies["row", w, h, du, dv] = copy

    pick_row, pick_col = iota((64, 64), 0), iota((64, 64), 1)
    picks = one_hot((pick_col // 4 == pick_row % 16) & (pick_col % 4 == pick_row // 16))

    def unpack(w):
        for j in range(4 * w, 4 * w + 4):
            if j > 0:
                z_copies[j].wait_recv()
        rows = dot(picks, landed[4 * w : 4 * w + 4].reshape(64, QUARTER)).astype(BF16)
        low = 4 * w * ROWS
        for i in range(4):
            xs[0, low : low + ROWS, i * QUARTER : (i + 1) * QUARTER] = rows[
                i * ROWS : (i + 1) * ROWS
            ]

    def own(w, h, axis, step):
        gather(w, h, axis, step, 0, 0)

    def far(w, h):
        gather(w, h, 0, 2, 0, 0)

    def across(w, h, u, step):
        arrived(("row", w, h, u, 0))
        gather(w, h, 1, step, u, 0)

    def pass_on(w, h, u):
        arrived(("row", w, h, u, 1))
        gather(w, h, 1, 1, u, 1)

    def experts(_, v):
        if v == FIRST_BLOCK:
            for wc in weight_loads:
                wc.wait()
        for w in range(2):
            for h in range(PIECES):
                for u in range(4):
                    if (u, v) != (0, 0):
                        arrived(("row", w, h, u, v))
        for n in range(2):
            cols = slice(n * 256, (n + 1) * 256)
            gate = dot(xs[v], wg[:, cols])
            up = dot(xs[v], wu[:, cols])
            hidden[:, cols] = (gate / (1.0 + jnp.exp(-gate)) * up).astype(BF16)
        for n in range(6):
            cols = slice(n * 512, (n + 1) * 512)
            parts[v, :, cols] = dot(hidden[...], wd[:, cols]).astype(BF16)

    def send_sum(kind, w, h, u, axis, step, src):
        buf = (r1, r2, r3, r4, r5, r6)[kind - 1]
        cols = pl.ds(h * SPAN, SPAN)
        if kind <= 3:
            dst, number = buf.at[w, u, :, cols], ((kind * 2 - 2 + w) * 4 + u) * PIECES + h
        else:
            dst, number = buf.at[w, :, cols], (24 + (kind - 4) * 2 + w) * PIECES + h
        copy = pltpu.make_async_remote_copy(
            src_ref=src, dst_ref=dst,
            send_sem=rs_send.at[number], recv_sem=rs_recv.at[number],
            device_id=at(w, axis, step), device_id_type=MESH,
        )
        copy.start()
        copies[kind, w, h, u if kind <= 3 else 0] = copy

    def landing(kind, w, h, u):
        arrived((kind, w, h, u))
        buf = (r1, r2, r3, r4, r5, r6)[kind - 1]
        cols = slice(h * SPAN, (h + 1) * SPAN)
        return (buf[w, u, :, cols] if kind <= 3 else buf[w, :, cols]).astype(F32)

    def sum_direct(w, h, u):
        send_sum(2, w, h, u, 1, 1, piece(parts, w, h, u, 3))

    def sum_opposite(w, h, u):
        send_sum(1, w, h, u, 1, -1, piece(parts, w, h, u, 2))

    def sum_pass(w, h, u):
        mine = piece(parts, w, h, u, 1)
        mine[...] = (mine[...].astype(F32) + landing(1, w, h, u)).astype(BF16)
        send_sum(3, w, h, u, 1, -1, mine)

    def sum_line(w, h, u):
        mine = piece(parts, w, h, u, 0)
        mine[...] = (
            mine[...].astype(F32) + landing(2, w, h, u) + landing(3, w, h, u)
        ).astype(BF16)
        if u > 0:
            send_sum(3 + u, w, h, u, 0, (-1, 2, 1)[u - 1], mine)

    returns = {}
    spreads = one_hot((pick_row // 4 == pick_col % 16) & (pick_row % 4 == pick_col // 16))

    def give_back(w, h):
        total = (
            piece(parts, w, h, 0, 0)[...].astype(F32)
            + landing(4, w, h, 0)
            + landing(5, w, h, 0)
            + landing(6, w, h, 0)
        ).astype(BF16)
        halves = range(2) if PIECES == 1 else (h,)
        for half in halves:
            low = half * HALF if PIECES == 1 else 0
            rows = jnp.concatenate(
                [total[:, low + i * EIGHTH : low + (i + 1) * EIGHTH] for i in range(4)], axis=0
            )
            rows = dot(spreads, rows)
            back[half, 4 * w : 4 * w + 4] = rows.astype(BF16).reshape(4, ROWS, EIGHTH)
        for j in (3, 2, 1, 0) if w == 0 else (7, 6, 5, 4):
            for half in halves:
                number = j * 2 + half
                copy = pltpu.make_async_remote_copy(
                    src_ref=back.at[half, j], dst_ref=home.at[j, role],
                    send_sem=ret_send.at[number], recv_sem=ret_recv.at[j * 2 + role],
                    device_id=at_z(-turn * OFFSETS[j], half), device_id_type=MESH,
                )
                returns[j, half] = copy
                if j > 0:
                    copy.start()
            if j == 0 and sum(key[0] == 0 for key in returns) == 2:
                copy = pltpu.make_async_remote_copy(
                    src_ref=back.at[1 - role, 0], dst_ref=home.at[0, role],
                    send_sem=ret_send.at[0], recv_sem=ret_recv.at[0],
                    device_id=at_z(0, 1 - role), device_id_type=MESH,
                )
                copy.start()
                sibling.append(copy)
                home[0, role] = back[role, 0]

    sibling = []

    def mix_table():
        row, col = iota((128, 256), 0), iota((128, 256), 1)
        core = (col // 16) % 2
        expert = (z + (1 - 2 * core) * offset_of(col // 32) + 8) % 8
        names = [
            jnp.sum(jnp.where(diagonal, ids[k : k + 1, :], 0), axis=1, keepdims=True)
            for k in range(2)
        ]
        names = [jnp.concatenate([name] * 8, axis=0) for name in names]
        hit = (names[0] == expert) | (names[1] == expert)
        trow, tcol = iota((128, 128), 0), iota((128, 128), 1)
        before = one_hot((trow // 16 == tcol // 16) & (tcol < trow))
        rank = dot(before, one_hot(hit))
        fits = (rank == ((col // 4) % 8).astype(F32)) & (col % 4 == (row // 16) % 4)
        named = jnp.where(row < 64, names[0], names[1]) == expert
        table[...] = one_hot(named & fits)

    def mix(w, so_far):
        for j in range(4 * w, 4 * w + 4):
            for core in range(2):
                if j == 0 and core == 0:
                    sibling[0].wait_recv()
                elif j > 0:
                    pltpu.make_async_remote_copy(
                        src_ref=back.at[core, j], dst_ref=home.at[j, core],
                        send_sem=ret_send.at[j * 2 + core], recv_sem=ret_recv.at[j * 2 + core],
                        device_id=at_z(turn, role), device_id_type=MESH,
                    ).wait_recv()
        rows = home[4 * w : 4 * w + 4].reshape(128, EIGHTH)
        terms = dot(table[:, 128 * w : 128 * w + 128], rows)
        new = []
        for i in range(4):
            total = so_far[i] if so_far else 0.0
            for k in range(2):
                low = (k * 4 + i) * ROWS
                total = total + terms[low : low + ROWS] * weight[k]
            new.append(total)
        return new

    weight = [
        jnp.sum(jnp.where(diagonal, gates[k : k + 1, :], 0.0), axis=1, keepdims=True)
        for k in range(2)
    ]

    steps = {
        "unpack": unpack, "own": own, "far": far, "across": across, "pass": pass_on,
        "experts": experts, "direct": sum_direct, "opposite": sum_opposite, "sum": sum_pass,
        "line": sum_line, "give": give_back,
    }
    for name, *where in ORDER:
        if name == "give" and not returns:
            mix_table()
        steps[name](*where)
    mixed = mix(MIX[1], mix(MIX[0], None))
    for i in range(4):
        out_ref[:, i * EIGHTH : (i + 1) * EIGHTH] = mixed[i].astype(BF16)

    for copy in list(z_copies.values()) + list(copies.values()) + sibling:
        copy.wait_send()
    for (j, _), copy in returns.items():
        if j > 0:
            copy.wait_send()


def local(
    queries, cached_keys, cached_values, lengths, norm_gain,
    expert_ids, gates, gate_proj, up_proj, down_proj,
):
    vmem = pl.BlockSpec(memory_space=pltpu.VMEM)
    smem = pl.BlockSpec(memory_space=pltpu.SMEM)
    hbm = pl.BlockSpec(memory_space=pl.ANY)
    dma = pltpu.SemaphoreType.DMA
    return pl.pallas_call(
        kernel,
        out_shape=jax.ShapeDtypeStruct((REQUESTS, HALF), BF16),
        in_specs=[hbm, hbm, hbm, smem, hbm, hbm, hbm, hbm, hbm, hbm],
        out_specs=vmem,
        scratch_shapes=[
            pltpu.VMEM((REQUESTS, MODEL_WIDTH), BF16),
            pltpu.VMEM((1, MODEL_WIDTH), F32),
            pltpu.VMEM((2, REQUESTS), jnp.int32),
            pltpu.VMEM((2, REQUESTS), F32),
            pltpu.VMEM((REQUESTS, POSITIONS, WIDE), BF16),
            pltpu.VMEM((REQUESTS, POSITIONS, WIDE), BF16),
            pltpu.VMEM((MODEL_WIDTH, WIDE), BF16),
            pltpu.VMEM((MODEL_WIDTH, WIDE), BF16),
            pltpu.VMEM((WIDE, MODEL_WIDTH), BF16),
            pltpu.VMEM((REQUESTS * QUERY_HEADS, HEAD_WIDTH), F32),
            pltpu.VMEM((REQUESTS * QUERY_HEADS, HEAD_WIDTH), F32),
            pltpu.VMEM((REQUESTS * QUERY_HEADS, HEAD_WIDTH), F32),
            pltpu.VMEM((8, ROWS, QUARTER), BF16),
            pltpu.VMEM((8, ROWS, QUARTER), BF16),
            pltpu.VMEM((4, 128, MODEL_WIDTH), BF16),
            pltpu.VMEM((128, WIDE), BF16),
            pltpu.VMEM((4, 128, MODEL_WIDTH), BF16),
            pltpu.VMEM((2, 4, ROWS, MODEL_WIDTH), BF16),
            pltpu.VMEM((2, 4, ROWS, MODEL_WIDTH), BF16),
            pltpu.VMEM((2, 4, ROWS, MODEL_WIDTH), BF16),
            pltpu.VMEM((2, ROWS, MODEL_WIDTH), BF16),
            pltpu.VMEM((2, ROWS, MODEL_WIDTH), BF16),
            pltpu.VMEM((2, ROWS, MODEL_WIDTH), BF16),
            pltpu.VMEM((2, 8, ROWS, EIGHTH), BF16),
            pltpu.VMEM((8, 2, ROWS, EIGHTH), BF16),
            pltpu.VMEM((128, 256), BF16),
            dma((4,)), dma((8,)), dma((3,)), dma((8,)), dma((8,)), dma((32 * PIECES,)), dma((32 * PIECES,)),
            dma((30 * PIECES,)), dma((30 * PIECES,)), dma((16,)), dma((16,)),
        ],
        compiler_params=pltpu.CompilerParams(
            collective_id=0, has_side_effects=True, vmem_limit_bytes=56 * 1024 * 1024
        ),
        cost_estimate=pl.CostEstimate(
            flops=5_000_000_000, bytes_accessed=14_000_000, transcendentals=400_000
        ),
    )(
        queries, cached_keys, cached_values, lengths, norm_gain.reshape(1, MODEL_WIDTH),
        expert_ids.T, gates.T, gate_proj, up_proj, down_proj,
    )


def solution(mesh):
    placed = (
        P(("grp", "tp"), None),
        P(("grp", "tp"), None, None),
        P(("grp", "tp"), None, None),
        P(("grp", "tp")),
        P(),
        P(("grp", "tp"), None),
        P(("grp", "tp"), None),
        P("grp", None, "tp"),
        P("grp", None, "tp"),
        P("grp", "tp", None),
    )
    return jax.shard_map(
        local, mesh=mesh, in_specs=placed, out_specs=P(("grp", "tp"), "role"), check_vma=False
    )
```

time: 69.7 us -> 66.5 us (0.954)
  local copies, waits for them, and re-layouts: 4.12 us -> 1.42 us
    unnamed x3 -> x1, local copies, waits for them, and re-layouts: 4.12 us -> 1.42 us
where the time goes in v2:
time: 66.5 us; the launch traced here: 66.3 us
  Pallas kernels  64.9 us (98%)
  local copies, waits for them, and re-layouts  1.42 us (2%)
    pallas_call x1, Pallas kernels, local(): pl.pallas_call(kernel, out_shape=jax.ShapeDtypeStruct((REQUESTS, HALF), B...  64.9 us
    unnamed x1, local copies, waits for them, and re-layouts  1.42 us

profile of v2, /device:TPU:1, one launch (start us, length us, event | category | flops | bytes accessed | tf_op | source)
XLA Modules:
  0.0 66.3 jit_solution(13986959769271959259)
XLA Ops:
  0.0 64.9 %shard_map.100 = bf16[16,1536]{1,0:T(8,128)(2,1)} custom-call(bf16[16,3072]{1,0:T(8,128)(2,1)} %q_hbm.1, bf16[16,128,512]{2,1,0:T(8,128)(2,1)} %k_hbm.1, bf16[16,128,512]{2,1,0:T(8,128)(2,1)} %v_hbm.1, s32[16]{0:T(128)} %len_ref.1, f32[1,3072]{1,0:T(1,128)} %bitcast.3, s32[2,16]{1,0:T(2,128)} %bitcast.4, f32[2,16]{1,0:T(2,128)} %bitcast.5, ...), custom_call_target="tpu_custom_call" | custom-call | flops 5000000000 | bytes 14000000 | tf_op jit(solution)/shard_map/pallas_call | solution.py:424
  64.9 1.4 %copy.12 = bf16[16,1536]{1,0:T(8,128)(2,1)} copy(bf16[16,1536]{1,0:T(8,128)(2,1)} %shard_map.100) | data formatting | bytes 98304

commit v3 on v2

v3 whole, which is shorter than its diff:
```python
import functools
import math

import jax
import jax.numpy as jnp
from jax import lax
from jax.experimental import pallas as pl
from jax.experimental.pallas import tpu as pltpu
from jax.sharding import PartitionSpec as P

HEAD_WIDTH = 128
QUERY_HEADS = 24
KEY_VALUE_HEADS = 4
MODEL_WIDTH = 3072
REQUESTS = 16
POSITIONS = 128
WIDE = 512
QUARTER = 768
HALF = 1536
EIGHTH = 384
ROWS = 16
OFFSETS = (0, 1, -1, 2, -2, 3, -3, 4)
MIX = (1, 0)
FIRST_BLOCK = 0
ORDER = (
    ("unpack", 0), ("own", 0, 0, 1), ("own", 0, 0, -1), ("own", 0, 1, 1), ("own", 0, 1, -1),
    ("far", 0), ("unpack", 1), ("own", 1, 0, 1), ("own", 1, 0, -1), ("own", 1, 1, 1),
    ("own", 1, 1, -1), ("far", 1), ("across", 0, 1, 1), ("across", 0, 1, -1), ("across", 1, 1, 1),
    ("across", 1, 1, -1), ("across", 0, 3, 1), ("across", 0, 3, -1), ("across", 1, 3, 1),
    ("across", 1, 3, -1), ("pass", 0, 0), ("pass", 1, 0), ("across", 0, 2, 1),
    ("across", 0, 2, -1), ("across", 1, 2, 1), ("across", 1, 2, -1), ("experts", 0),
    ("pass", 0, 1), ("pass", 1, 1), ("pass", 0, 3), ("pass", 1, 3), ("pass", 0, 2),
    ("pass", 1, 2), ("experts", 3), ("direct", 1, 2), ("direct", 0, 2), ("direct", 1, 1),
    ("direct", 0, 1), ("direct", 1, 3), ("direct", 0, 3), ("direct", 1, 0), ("direct", 0, 0),
    ("experts", 1), ("experts", 2), ("opposite", 1, 2), ("opposite", 0, 2), ("opposite", 1, 1),
    ("opposite", 0, 1), ("opposite", 1, 3), ("opposite", 0, 3), ("opposite", 1, 0),
    ("opposite", 0, 0), ("sum", 1, 2), ("sum", 0, 2), ("sum", 1, 1), ("sum", 0, 1), ("sum", 1, 3),
    ("sum", 0, 3), ("sum", 1, 0), ("sum", 0, 0), ("line", 1, 2), ("line", 0, 2), ("line", 1, 1),
    ("line", 0, 1), ("line", 1, 3), ("line", 0, 3), ("line", 1, 0), ("line", 0, 0), ("give", 1),
    ("give", 0),
)
MESH = pl.DeviceIdType.MESH
F32 = jnp.float32
BF16 = jnp.bfloat16


def iota(shape, axis):
    return lax.broadcasted_iota(jnp.int32, shape, axis)


def one_hot(mask):
    return jnp.where(mask, 1.0, 0.0).astype(BF16)


def dot(a, b):
    return jnp.dot(a, b, preferred_element_type=F32)


def offset_of(index):
    step = (index + 1) // 2
    return jnp.where(index % 2 == 1, step, -step)


def kernel(
    q_hbm, k_hbm, v_hbm, len_hbm, gain_hbm, ids_hbm, gates_hbm, wg_hbm, wu_hbm, wd_hbm,
    out_ref,
    q_buf, gain, ids, gates, k_buf, v_buf, wg, wu, wd, q_rows, s_rows, c_rows,
    packed, landed, xs, hidden, parts, r1, r2, r3, back, home, table, lengths,
    local_sem, sent, z_recv, ag_recv, rs_recv, ret_recv,
):
    role = lax.axis_index("role")
    z = lax.axis_index("grp")
    t = lax.axis_index("tp")
    x, y = t % 4, t // 4
    turn = 1 - 2 * role

    def at(w, axis, step):
        along_x = int(axis == w)
        col = (x + step * turn * along_x + 4) % 4
        row = (y + step * turn * (1 - along_x) + 4) % 4
        return (role, z, row * 4 + col)

    def at_z(step, core):
        return (core, (z + step + 8) % 8, t)

    barrier = pltpu.get_barrier_semaphore()
    partners = [at(0, a, step) for a in (0, 1) for step in (1, -1, 2)] + [at_z(0, 1 - role)]
    for step in OFFSETS[1:]:
        partners += [at_z(step, role), at_z(step, 1 - role)]
    for partner in partners:
        pl.semaphore_signal(barrier, inc=1, device_id=partner, device_id_type=MESH)

    small = [
        pltpu.make_async_copy(src, dst, local_sem.at[i])
        for i, (src, dst) in enumerate(
            ((q_hbm, q_buf), (len_hbm, lengths), (ids_hbm, ids), (gain_hbm, gain),
             (gates_hbm, gates))
        )
    ]
    loads = []
    for i in range(4):
        rows = pl.ds(4 * i, 4)
        loads.append((
            pltpu.make_async_copy(k_hbm.at[rows], k_buf.at[rows], local_sem.at[8 + i]),
            pltpu.make_async_copy(v_hbm.at[rows], v_buf.at[rows], local_sem.at[12 + i]),
        ))
    weight_loads = [
        pltpu.make_async_copy(src.at[0], dst, local_sem.at[5 + i])
        for i, (src, dst) in enumerate(((wg_hbm, wg), (wu_hbm, wu), (wd_hbm, wd)))
    ]
    small[0].start()
    small[1].start()
    for kc, _ in loads:
        kc.start()
    for _, vc in loads:
        vc.start()
    for copy in small[2:]:
        copy.start()

    small[0].wait()
    for h in range(QUERY_HEADS):
        q_rows[pl.ds(h, REQUESTS, stride=QUERY_HEADS), :] = q_buf[
            :, h * HEAD_WIDTH : (h + 1) * HEAD_WIDTH
        ].astype(F32)
    small[1].wait()
    group = iota((QUERY_HEADS, HEAD_WIDTH), 0) // (QUERY_HEADS // KEY_VALUE_HEADS)
    place = iota((QUERY_HEADS, POSITIONS), 1)
    scale = 1.0 / math.sqrt(HEAD_WIDTH)
    for r in range(REQUESTS):
        if r % 4 == 0:
            loads[r // 4][0].wait()
        own = q_rows[r * QUERY_HEADS : (r + 1) * QUERY_HEADS, :]
        spread = jnp.concatenate(
            [jnp.where(group == j, own, 0.0) for j in range(KEY_VALUE_HEADS)], axis=1
        ).astype(BF16)
        scores = lax.dot_general(
            spread, k_buf[r], (((1,), (1,)), ((), ())), preferred_element_type=F32
        )
        s_rows[r * QUERY_HEADS : (r + 1) * QUERY_HEADS, :] = jnp.where(
            place < lengths[r], scores * scale, -jnp.inf
        )
    for wc in weight_loads:
        wc.start()
    scores = s_rows[...]
    raised = jnp.exp(scores - jnp.max(scores, axis=1, keepdims=True))
    s_rows[...] = raised / jnp.sum(raised, axis=1, keepdims=True)
    for r in range(REQUESTS):
        if r % 4 == 0:
            loads[r // 4][1].wait()
        weights = s_rows[r * QUERY_HEADS : (r + 1) * QUERY_HEADS, :].astype(BF16)
        mixed = dot(weights, v_buf[r])
        own = jnp.where(group == 0, mixed[:, :HEAD_WIDTH], 0.0)
        for j in range(1, KEY_VALUE_HEADS):
            own = jnp.where(group == j, mixed[:, j * HEAD_WIDTH : (j + 1) * HEAD_WIDTH], own)
        c_rows[r * QUERY_HEADS : (r + 1) * QUERY_HEADS, :] = own
    for copy in small[2:]:
        copy.wait()
    heads = [
        c_rows[pl.ds(h, REQUESTS, stride=QUERY_HEADS), :] for h in range(QUERY_HEADS)
    ]
    squares = heads[0] * heads[0]
    for head in heads[1:]:
        squares = squares + head * head
    mean_square = jnp.sum(squares, axis=1, keepdims=True) / MODEL_WIDTH
    norm = lax.rsqrt(mean_square + 1e-05)
    expert_in = [
        head * norm * gain[:, h * HEAD_WIDTH : (h + 1) * HEAD_WIDTH]
        for h, head in enumerate(heads)
    ]
    stacked = jnp.concatenate(
        [jnp.concatenate(expert_in[6 * i : 6 * i + 6], axis=1) for i in range(4)], axis=0
    ).astype(BF16)

    diagonal = iota((16, 16), 0) == iota((16, 16), 1)
    first = jnp.concatenate([ids[0:1, :]] * 4, axis=1)
    second = jnp.concatenate([ids[1:2, :]] * 4, axis=1)
    row, col = iota((128, 64), 0), iota((128, 64), 1)
    expert = (z + turn * offset_of(row // 16) + 8) % 8
    hit = (first == expert) | (second == expert)
    trow, tcol = iota((64, 64), 0), iota((64, 64), 1)
    earlier = (trow // 16 == tcol // 16) & (trow % 16 < tcol % 16)
    rank = dot(one_hot(hit), one_hot(earlier))
    slot = ((row // 4) % 4 + 4 * role).astype(F32)
    chosen = one_hot(hit & (rank == slot) & (row % 4 == col // 16))
    packets = dot(chosen, stacked).astype(BF16)
    packed[...] = packets.reshape(8, ROWS, QUARTER)

    pl.semaphore_wait(barrier, len(partners))

    def landing(ref, sem):
        pltpu.make_async_copy(ref, ref, sem).wait()

    for j in (1, 2, 3, 7, 5, 6, 4):
        pltpu.make_async_remote_copy(
            src_ref=packed.at[j], dst_ref=landed.at[j],
            send_sem=sent.at[0], recv_sem=z_recv.at[j // 4],
            device_id=at_z(turn * OFFSETS[j], role), device_id_type=MESH,
        ).start()
    landed[0] = packets[:ROWS]

    def block(ref, w, u, v):
        return ref.at[pl.ds((v * 8 + w * 4 + u) * ROWS, ROWS), :]

    def gather(w, axis, step, u, v):
        du, dv = ((u + step) % 4, v) if axis == 0 else (u, (v + step) % 4)
        number = (w * 3 + du - 1, 6 + w * 4 + du, 14, 15)[dv]
        pltpu.make_async_remote_copy(
            src_ref=block(xs, w, u, v), dst_ref=block(xs, w, du, dv),
            send_sem=sent.at[1], recv_sem=ag_recv.at[number],
            device_id=at(w, axis, step), device_id_type=MESH,
        ).start()

    seen = set()

    def arrived(w, u, v):
        if (w, u, v) not in seen:
            seen.add((w, u, v))
            landing(block(xs, w, u, v), ag_recv.at[w * 3 + u - 1 if v == 0 else 6 + w * 4 + u])

    pick_row, pick_col = iota((64, 64), 0), iota((64, 64), 1)
    picks = one_hot((pick_col // 4 == pick_row % 16) & (pick_col % 4 == pick_row // 16))

    def unpack(w):
        first = max(4 * w, 1)
        landing(landed.at[pl.ds(first, 4 * w + 4 - first)], z_recv.at[w])
        rows = dot(picks, landed[4 * w : 4 * w + 4].reshape(64, QUARTER)).astype(BF16)
        low = 4 * w * ROWS
        for i in range(4):
            xs[low : low + ROWS, i * QUARTER : (i + 1) * QUARTER] = rows[
                i * ROWS : (i + 1) * ROWS
            ]

    def own(w, axis, step):
        gather(w, axis, step, 0, 0)

    def far(w):
        gather(w, 0, 2, 0, 0)

    def across(w, u, step):
        arrived(w, u, 0)
        gather(w, 1, step, u, 0)

    def pass_on(w, u):
        arrived(w, u, 1)
        gather(w, 1, 1, u, 1)

    def experts(v):
        if v == FIRST_BLOCK:
            for wc in weight_loads:
                wc.wait()
        low = v * 128
        if v > 1:
            landing(xs.at[pl.ds(low, 128)], ag_recv.at[12 + v])
        else:
            for w in range(2):
                for u in range(1 - v, 4):
                    arrived(w, u, v)
        for n in range(2):
            cols = slice(n * 256, (n + 1) * 256)
            gate = dot(xs[low : low + 128], wg[:, cols])
            up = dot(xs[low : low + 128], wu[:, cols])
            hidden[:, cols] = (gate / (1.0 + jnp.exp(-gate)) * up).astype(BF16)
        for n in range(6):
            cols = slice(n * 512, (n + 1) * 512)
            parts[low : low + 128, cols] = dot(hidden[...], wd[:, cols]).astype(BF16)

    def send_sum(src, dst, number, w, axis, step):
        pltpu.make_async_remote_copy(
            src_ref=src, dst_ref=dst, send_sem=sent.at[2], recv_sem=rs_recv.at[number],
            device_id=at(w, axis, step), device_id_type=MESH,
        ).start()

    def sum_direct(w, u):
        send_sum(block(parts, w, u, 3), r2.at[w, u, 0], 8 + w * 4 + u, w, 1, 1)

    def sum_opposite(w, u):
        send_sum(block(parts, w, u, 2), r1.at[w, u], w * 4 + u, w, 1, -1)

    def sum_pass(w, u):
        landing(r1.at[w, u], rs_recv.at[w * 4 + u])
        mine = block(parts, w, u, 1)
        mine[...] = (mine[...].astype(F32) + r1[w, u].astype(F32)).astype(BF16)
        send_sum(mine, r2.at[w, u, 1], 8 + w * 4 + u, w, 1, -1)

    def sum_line(w, u):
        landing(r2.at[w, u], rs_recv.at[8 + w * 4 + u])
        mine = block(parts, w, u, 0)
        mine[...] = (
            mine[...].astype(F32) + r2[w, u, 0].astype(F32) + r2[w, u, 1].astype(F32)
        ).astype(BF16)
        if u > 0:
            send_sum(mine, r3.at[w, u - 1], 16 + w, w, 0, (-1, 2, 1)[u - 1])

    spreads = one_hot((pick_row // 4 == pick_col % 16) & (pick_row % 4 == pick_col // 16))

    def give_back(w):
        landing(r3.at[w], rs_recv.at[16 + w])
        total = block(parts, w, 0, 0)[...].astype(F32)
        for i in range(3):
            total = total + r3[w, i].astype(F32)
        total = total.astype(BF16)
        for half in range(2):
            cols = [half * HALF + i * EIGHTH for i in range(4)]
            rows = jnp.concatenate([total[:, low : low + EIGHTH] for low in cols], axis=0)
            low = half * 8 + 4 * w
            back[low : low + 4] = dot(spreads, rows).astype(BF16).reshape(4, ROWS, EIGHTH)
        for j in range(4 * w + 3, 4 * w - 1, -1):
            for other in range(2):
                half = role if other == 0 else 1 - role
                if j == 0 and other == 0:
                    home[0] = back[half * 8]
                    continue
                pltpu.make_async_remote_copy(
                    src_ref=back.at[half * 8 + j], dst_ref=home.at[j * 2 + other],
                    send_sem=sent.at[3], recv_sem=ret_recv.at[w],
                    device_id=at_z(-turn * OFFSETS[j], half), device_id_type=MESH,
                ).start()

    def mix_table():
        row, col = iota((128, 256), 0), iota((128, 256), 1)
        other = (col // 16) % 2
        core = role + other - 2 * role * other
        expert = (z + (1 - 2 * core) * offset_of(col // 32) + 8) % 8
        names = [
            jnp.sum(jnp.where(diagonal, ids[k : k + 1, :], 0), axis=1, keepdims=True)
            for k in range(2)
        ]
        names = [jnp.concatenate([name] * 8, axis=0) for name in names]
        hit = (names[0] == expert) | (names[1] == expert)
        trow, tcol = iota((128, 128), 0), iota((128, 128), 1)
        before = one_hot((trow // 16 == tcol // 16) & (tcol < trow))
        rank = dot(before, one_hot(hit))
        fits = (rank == (col % 16 // 4 + 4 * core).astype(F32)) & (col % 4 == (row // 16) % 4)
        named = jnp.where(row < 64, names[0], names[1]) == expert
        table[...] = one_hot(named & fits)

    def mix(w, so_far):
        first = max(8 * w, 1)
        landing(home.at[pl.ds(first, 8 * w + 8 - first)], ret_recv.at[w])
        rows = home[8 * w : 8 * w + 8].reshape(128, EIGHTH)
        terms = dot(table[:, 128 * w : 128 * w + 128], rows)
        new = []
        for i in range(4):
            total = so_far[i] if so_far else 0.0
            for k in range(2):
                low = (k * 4 + i) * ROWS
                total = total + terms[low : low + ROWS] * weight[k]
            new.append(total)
        return new

    weight = [
        jnp.sum(jnp.where(diagonal, gates[k : k + 1, :], 0.0), axis=1, keepdims=True)
        for k in range(2)
    ]

    steps = {
        "unpack": unpack, "own": own, "far": far, "across": across, "pass": pass_on,
        "experts": experts, "direct": sum_direct, "opposite": sum_opposite, "sum": sum_pass,
        "line": sum_line, "give": give_back,
    }
    mix_table()
    for name, *where in ORDER:
        steps[name](*where)
    mixed = mix(MIX[1], mix(MIX[0], None))
    for i in range(4):
        out_ref[:, i * EIGHTH : (i + 1) * EIGHTH] = mixed[i].astype(BF16)

    landing(packed.at[pl.ds(1, 7)], sent.at[0])
    landing(xs.at[pl.ds(0, 480)], sent.at[1])
    landing(parts.at[pl.ds(0, 480)], sent.at[2])
    landing(back.at[pl.ds(0, 15)], sent.at[3])


def local(
    queries, cached_keys, cached_values, lengths, norm_gain,
    expert_ids, gates, gate_proj, up_proj, down_proj,
):
    vmem = pl.BlockSpec(memory_space=pltpu.VMEM)
    hbm = pl.BlockSpec(memory_space=pl.ANY)
    dma = pltpu.SemaphoreType.DMA
    return pl.pallas_call(
        kernel,
        out_shape=jax.ShapeDtypeStruct((REQUESTS, HALF), BF16),
        in_specs=[hbm, hbm, hbm, hbm, hbm, hbm, hbm, hbm, hbm, hbm],
        out_specs=vmem,
        scratch_shapes=[
            pltpu.VMEM((REQUESTS, MODEL_WIDTH), BF16),
            pltpu.VMEM((1, MODEL_WIDTH), F32),
            pltpu.VMEM((2, REQUESTS), jnp.int32),
            pltpu.VMEM((2, REQUESTS), F32),
            pltpu.VMEM((REQUESTS, POSITIONS, WIDE), BF16),
            pltpu.VMEM((REQUESTS, POSITIONS, WIDE), BF16),
            pltpu.VMEM((MODEL_WIDTH, WIDE), BF16),
            pltpu.VMEM((MODEL_WIDTH, WIDE), BF16),
            pltpu.VMEM((WIDE, MODEL_WIDTH), BF16),
            pltpu.VMEM((REQUESTS * QUERY_HEADS, HEAD_WIDTH), F32),
            pltpu.VMEM((REQUESTS * QUERY_HEADS, HEAD_WIDTH), F32),
            pltpu.VMEM((REQUESTS * QUERY_HEADS, HEAD_WIDTH), F32),
            pltpu.VMEM((8, ROWS, QUARTER), BF16),
            pltpu.VMEM((8, ROWS, QUARTER), BF16),
            pltpu.VMEM((512, MODEL_WIDTH), BF16),
            pltpu.VMEM((128, WIDE), BF16),
            pltpu.VMEM((512, MODEL_WIDTH), BF16),
            pltpu.VMEM((2, 4, ROWS, MODEL_WIDTH), BF16),
            pltpu.VMEM((2, 4, 2, ROWS, MODEL_WIDTH), BF16),
            pltpu.VMEM((2, 3, ROWS, MODEL_WIDTH), BF16),
            pltpu.VMEM((16, ROWS, EIGHTH), BF16),
            pltpu.VMEM((16, ROWS, EIGHTH), BF16),
            pltpu.VMEM((128, 256), BF16),
            pltpu.SMEM((REQUESTS,), jnp.int32),
            dma((16,)), dma((4,)), dma((2,)), dma((16,)), dma((18,)), dma((2,)),
        ],
        compiler_params=pltpu.CompilerParams(
            collective_id=0, has_side_effects=True, vmem_limit_bytes=56 * 1024 * 1024
        ),
        cost_estimate=pl.CostEstimate(
            flops=5_000_000_000, bytes_accessed=14_000_000, transcendentals=400_000
        ),
    )(
        queries, cached_keys, cached_values, lengths, norm_gain.reshape(1, MODEL_WIDTH),
        expert_ids.T, gates.T, gate_proj, up_proj, down_proj,
    )


def solution(mesh):
    placed = (
        P(("grp", "tp"), None),
        P(("grp", "tp"), None, None),
        P(("grp", "tp"), None, None),
        P(("grp", "tp")),
        P(),
        P(("grp", "tp"), None),
        P(("grp", "tp"), None),
        P("grp", None, "tp"),
        P("grp", None, "tp"),
        P("grp", "tp", None),
    )
    return jax.shard_map(
        local, mesh=mesh, in_specs=placed, out_specs=P(("grp", "tp"), "role"), check_vma=False
    )
```

time: 66.5 us -> 63.7 us (0.958)
  Pallas kernels: 64.9 us -> 62.1 us
    pallas_call x1, Pallas kernels: 64.9 us -> 62.1 us  [local(): pl.pallas_call(kernel, out_shape=jax.ShapeDtypeStruct((REQUESTS, HALF), B...]
where the time goes in v3:
time: 63.7 us; the launch traced here: 63.5 us
  Pallas kernels  62.1 us (97%)
  local copies, waits for them, and re-layouts  1.42 us (2%)
    pallas_call x1, Pallas kernels, local(): pl.pallas_call(kernel, out_shape=jax.ShapeDtypeStruct((REQUESTS, HALF), B...  62.1 us
    unnamed x1, local copies, waits for them, and re-layouts  1.42 us

profile of v3, /device:TPU:1, one launch (start us, length us, event | category | flops | bytes accessed | tf_op | source)
XLA Modules:
  0.0 63.5 jit_solution(3799386291800396106)
XLA Ops:
  0.0 62.1 %shard_map.100 = bf16[16,1536]{1,0:T(8,128)(2,1)} custom-call(bf16[16,3072]{1,0:T(8,128)(2,1)} %q_hbm.1, bf16[16,128,512]{2,1,0:T(8,128)(2,1)} %k_hbm.1, bf16[16,128,512]{2,1,0:T(8,128)(2,1)} %v_hbm.1, s32[16]{0:T(128)} %len_hbm.1, f32[1,3072]{1,0:T(1,128)} %bitcast.3, s32[2,16]{1,0:T(2,128)} %bitcast.4, f32[2,16]{1,0:T(2,128)} %bitcast.5, ...), custom_call_target="tpu_custom_call" | custom-call | flops 5000000000 | bytes 14000000 | tf_op jit(solution)/shard_map/pallas_call | solution.py:381
  62.1 1.4 %copy.12 = bf16[16,1536]{1,0:T(8,128)(2,1)} copy(bf16[16,1536]{1,0:T(8,128)(2,1)} %shard_map.100) | data formatting | bytes 98304

commit v4 on v3

--- a/solution.py
+++ b/solution.py
@@ -24,20 +24,30 @@
 FIRST_BLOCK = 0
 ORDER = (
     ("unpack", 0), ("own", 0, 0, 1), ("own", 0, 0, -1), ("own", 0, 1, 1), ("own", 0, 1, -1),
-    ("far", 0), ("unpack", 1), ("own", 1, 0, 1), ("own", 1, 0, -1), ("own", 1, 1, 1),
-    ("own", 1, 1, -1), ("far", 1), ("across", 0, 1, 1), ("across", 0, 1, -1), ("across", 1, 1, 1),
+    ("unpack", 1), ("own", 1, 0, 1), ("own", 1, 0, -1), ("own", 1, 1, 1), ("own", 1, 1, -1),
+    ("far", 0), ("across", 0, 1, 1), ("across", 0, 1, -1), ("far", 1), ("across", 1, 1, 1),
     ("across", 1, 1, -1), ("across", 0, 3, 1), ("across", 0, 3, -1), ("across", 1, 3, 1),
     ("across", 1, 3, -1), ("pass", 0, 0), ("pass", 1, 0), ("across", 0, 2, 1),
     ("across", 0, 2, -1), ("across", 1, 2, 1), ("across", 1, 2, -1), ("experts", 0),
-    ("pass", 0, 1), ("pass", 1, 1), ("pass", 0, 3), ("pass", 1, 3), ("pass", 0, 2),
-    ("pass", 1, 2), ("experts", 3), ("direct", 1, 2), ("direct", 0, 2), ("direct", 1, 1),
-    ("direct", 0, 1), ("direct", 1, 3), ("direct", 0, 3), ("direct", 1, 0), ("direct", 0, 0),
-    ("experts", 1), ("experts", 2), ("opposite", 1, 2), ("opposite", 0, 2), ("opposite", 1, 1),
-    ("opposite", 0, 1), ("opposite", 1, 3), ("opposite", 0, 3), ("opposite", 1, 0),
-    ("opposite", 0, 0), ("sum", 1, 2), ("sum", 0, 2), ("sum", 1, 1), ("sum", 0, 1), ("sum", 1, 3),
-    ("sum", 0, 3), ("sum", 1, 0), ("sum", 0, 0), ("line", 1, 2), ("line", 0, 2), ("line", 1, 1),
-    ("line", 0, 1), ("line", 1, 3), ("line", 0, 3), ("line", 1, 0), ("line", 0, 0), ("give", 1),
-    ("give", 0),
+    ("down", 0, 0), ("down", 0, 1), ("pass", 0, 1), ("pass", 1, 1), ("pass", 0, 3),
+    ("pass", 1, 3), ("pass", 0, 2), ("pass", 1, 2), ("experts", 3), ("down", 3, 0),
+    ("down", 3, 1), ("direct", 1, 0, 2), ("direct", 0, 0, 2), ("direct", 1, 0, 1),
+    ("direct", 0, 0, 1), ("direct", 1, 0, 3), ("direct", 0, 0, 3), ("direct", 1, 0, 0),
+    ("direct", 0, 0, 0), ("direct", 1, 1, 2), ("direct", 0, 1, 2), ("direct", 1, 1, 1),
+    ("direct", 0, 1, 1), ("direct", 1, 1, 3), ("direct", 0, 1, 3), ("direct", 1, 1, 0),
+    ("direct", 0, 1, 0), ("experts", 1), ("down", 1, 0), ("down", 1, 1), ("experts", 2),
+    ("down", 2, 0), ("opposite", 1, 0, 2), ("opposite", 0, 0, 2), ("opposite", 1, 0, 1),
+    ("opposite", 0, 0, 1), ("opposite", 1, 0, 3), ("opposite", 0, 0, 3), ("opposite", 1, 0, 0),
+    ("opposite", 0, 0, 0), ("down", 2, 1), ("opposite", 1, 1, 2), ("opposite", 0, 1, 2),
+    ("opposite", 1, 1, 1), ("opposite", 0, 1, 1), ("opposite", 1, 1, 3), ("opposite", 0, 1, 3),
+    ("opposite", 1, 1, 0), ("opposite", 0, 1, 0), ("sum", 1, 0, 2), ("sum", 0, 0, 2),
+    ("sum", 1, 0, 1), ("sum", 0, 0, 1), ("sum", 1, 0, 3), ("sum", 0, 0, 3), ("sum", 1, 0, 0),
+    ("sum", 0, 0, 0), ("sum", 1, 1, 2), ("sum", 0, 1, 2), ("sum", 1, 1, 1), ("sum", 0, 1, 1),
+    ("sum", 1, 1, 3), ("sum", 0, 1, 3), ("sum", 1, 1, 0), ("sum", 0, 1, 0), ("line", 1, 0, 2),
+    ("line", 0, 0, 2), ("line", 1, 0, 1), ("line", 0, 0, 1), ("line", 1, 0, 3), ("line", 0, 0, 3),
+    ("line", 1, 0, 0), ("line", 0, 0, 0), ("line", 1, 1, 2), ("line", 0, 1, 2), ("line", 1, 1, 1),
+    ("line", 0, 1, 1), ("line", 1, 1, 3), ("line", 0, 1, 3), ("line", 1, 1, 0), ("line", 0, 1, 0),
+    ("give", 1, 0), ("give", 0, 0), ("give", 1, 1), ("give", 0, 1),
 )
 MESH = pl.DeviceIdType.MESH
 F32 = jnp.float32
@@ -234,7 +244,8 @@
         gather(w, axis, step, 0, 0)
 
     def far(w):
-        gather(w, 0, 2, 0, 0)
+        arrived(w, 1, 0)
+        gather(w, 0, 1, 1, 0)
 
     def across(w, u, step):
         arrived(w, u, 0)
@@ -260,9 +271,16 @@
             gate = dot(xs[low : low + 128], wg[:, cols])
             up = dot(xs[low : low + 128], wu[:, cols])
             hidden[:, cols] = (gate / (1.0 + jnp.exp(-gate)) * up).astype(BF16)
-        for n in range(6):
+
+    def down(v, h):
+        low = v * 128
+        for n in range(3 * h, 3 * h + 3):
             cols = slice(n * 512, (n + 1) * 512)
             parts[low : low + 128, cols] = dot(hidden[...], wd[:, cols]).astype(BF16)
+
+
+    def half_block(w, h, u, v):
+        return block(parts, w, u, v).at[:, pl.ds(h * HALF, HALF)]
 
     def send_sum(src, dst, number, w, axis, step):
         pltpu.make_async_remote_copy(
@@ -270,51 +288,61 @@
             device_id=at(w, axis, step), device_id_type=MESH,
         ).start()
 
-    def sum_direct(w, u):
-        send_sum(block(parts, w, u, 3), r2.at[w, u, 0], 8 + w * 4 + u, w, 1, 1)
-
-    def sum_opposite(w, u):
-        send_sum(block(parts, w, u, 2), r1.at[w, u], w * 4 + u, w, 1, -1)
-
-    def sum_pass(w, u):
-        landing(r1.at[w, u], rs_recv.at[w * 4 + u])
-        mine = block(parts, w, u, 1)
-        mine[...] = (mine[...].astype(F32) + r1[w, u].astype(F32)).astype(BF16)
-        send_sum(mine, r2.at[w, u, 1], 8 + w * 4 + u, w, 1, -1)
-
-    def sum_line(w, u):
-        landing(r2.at[w, u], rs_recv.at[8 + w * 4 + u])
-        mine = block(parts, w, u, 0)
+    def sum_direct(w, h, u):
+        number = 16 + (w * 2 + h) * 4 + u
+        send_sum(half_block(w, h, u, 3), r2.at[w, h, u, 0], number, w, 1, 1)
+
+    def sum_opposite(w, h, u):
+        number = (w * 2 + h) * 4 + u
+        send_sum(half_block(w, h, u, 2), r1.at[w, h, u], number, w, 1, -1)
+
+    def sum_pass(w, h, u):
+        number = (w * 2 + h) * 4 + u
+        landing(r1.at[w, h, u], rs_recv.at[number])
+        mine = half_block(w, h, u, 1)
+        mine[...] = (mine[...].astype(F32) + r1[w, h, u].astype(F32)).astype(BF16)
+        send_sum(mine, r2.at[w, h, u, 1], 16 + number, w, 1, -1)
+
+    def sum_line(w, h, u):
+        landing(r2.at[w, h, u], rs_recv.at[16 + (w * 2 + h) * 4 + u])
+        mine = half_block(w, h, u, 0)
         mine[...] = (
-            mine[...].astype(F32) + r2[w, u, 0].astype(F32) + r2[w, u, 1].astype(F32)
+            mine[...].astype(F32) + r2[w, h, u, 0].astype(F32) + r2[w, h, u, 1].astype(F32)
         ).astype(BF16)
         if u > 0:
-            send_sum(mine, r3.at[w, u - 1], 16 + w, w, 0, (-1, 2, 1)[u - 1])
+            send_sum(mine, r3.at[w, h, u - 1], 32 + w * 2 + h, w, 0, (-1, 2, 1)[u - 1])
 
     spreads = one_hot((pick_row // 4 == pick_col % 16) & (pick_row % 4 == pick_col // 16))
 
-    def give_back(w):
-        landing(r3.at[w], rs_recv.at[16 + w])
-        total = block(parts, w, 0, 0)[...].astype(F32)
+    def give_back(w, h):
+        landing(r3.at[w, h], rs_recv.at[32 + w * 2 + h])
+        total = half_block(w, h, 0, 0)[...].astype(F32)
         for i in range(3):
-            total = total + r3[w, i].astype(F32)
+            total = total + r3[w, h, i].astype(F32)
         total = total.astype(BF16)
-        for half in range(2):
-            cols = [half * HALF + i * EIGHTH for i in range(4)]
-            rows = jnp.concatenate([total[:, low : low + EIGHTH] for low in cols], axis=0)
-            low = half * 8 + 4 * w
-            back[low : low + 4] = dot(spreads, rows).astype(BF16).reshape(4, ROWS, EIGHTH)
-        for j in range(4 * w + 3, 4 * w - 1, -1):
-            for other in range(2):
-                half = role if other == 0 else 1 - role
-                if j == 0 and other == 0:
-                    home[0] = back[half * 8]
-                    continue
-                pltpu.make_async_remote_copy(
-                    src_ref=back.at[half * 8 + j], dst_ref=home.at[j * 2 + other],
-                    send_sem=sent.at[3], recv_sem=ret_recv.at[w],
-                    device_id=at_z(-turn * OFFSETS[j], half), device_id_type=MESH,
-                ).start()
+        rows = jnp.concatenate(
+            [total[:, i * EIGHTH : (i + 1) * EIGHTH] for i in range(4)], axis=0
+        )
+        low = h * 8 + 4 * w
+        back[low : low + 4] = dot(spreads, rows).astype(BF16).reshape(4, ROWS, EIGHTH)
+        for j in range(4 * w + 3, max(4 * w, 1) - 1, -1):
+            other = role if h == 0 else 1 - role
+            pltpu.make_async_remote_copy(
+                src_ref=back.at[h * 8 + j], dst_ref=home.at[j * 2 + other],
+                send_sem=sent.at[3], recv_sem=ret_recv.at[w],
+                device_id=at_z(-turn * OFFSETS[j], h), device_id_type=MESH,
+            ).start()
+        if w == 0:
+            given.append(h)
+        if w == 0 and len(given) == 2:
+            home[0] = back[role * 8]
+            pltpu.make_async_remote_copy(
+                src_ref=back.at[(1 - role) * 8], dst_ref=home.at[1],
+                send_sem=sent.at[3], recv_sem=ret_recv.at[0],
+                device_id=at_z(0, 1 - role), device_id_type=MESH,
+            ).start()
+
+    given = []
 
     def mix_table():
         row, col = iota((128, 256), 0), iota((128, 256), 1)
@@ -355,7 +383,7 @@
 
     steps = {
         "unpack": unpack, "own": own, "far": far, "across": across, "pass": pass_on,
-        "experts": experts, "direct": sum_direct, "opposite": sum_opposite, "sum": sum_pass,
+        "experts": experts, "down": down, "direct": sum_direct, "opposite": sum_opposite, "sum": sum_pass,
         "line": sum_line, "give": give_back,
     }
     mix_table()
@@ -401,14 +429,14 @@
             pltpu.VMEM((512, MODEL_WIDTH), BF16),
             pltpu.VMEM((128, WIDE), BF16),
             pltpu.VMEM((512, MODEL_WIDTH), BF16),
-            pltpu.VMEM((2, 4, ROWS, MODEL_WIDTH), BF16),
-            pltpu.VMEM((2, 4, 2, ROWS, MODEL_WIDTH), BF16),
-            pltpu.VMEM((2, 3, ROWS, MODEL_WIDTH), BF16),
+            pltpu.VMEM((2, 2, 4, ROWS, HALF), BF16),
+            pltpu.VMEM((2, 2, 4, 2, ROWS, HALF), BF16),
+            pltpu.VMEM((2, 2, 3, ROWS, HALF), BF16),
             pltpu.VMEM((16, ROWS, EIGHTH), BF16),
             pltpu.VMEM((16, ROWS, EIGHTH), BF16),
             pltpu.VMEM((128, 256), BF16),
             pltpu.SMEM((REQUESTS,), jnp.int32),
-            dma((16,)), dma((4,)), dma((2,)), dma((16,)), dma((18,)), dma((2,)),
+            dma((16,)), dma((4,)), dma((2,)), dma((16,)), dma((36,)), dma((2,)),
         ],
         compiler_params=pltpu.CompilerParams(
             collective_id=0, has_side_effects=True, vmem_limit_bytes=56 * 1024 * 1024

time: 63.7 us -> 61.4 us (0.964)
  Pallas kernels: 62.1 us -> 59.9 us
    pallas_call x1, Pallas kernels: 62.1 us -> 59.9 us  [local(): pl.pallas_call(kernel, out_shape=jax.ShapeDtypeStruct((REQUESTS, HALF), B...]
where the time goes in v4:
time: 61.4 us; the launch traced here: 61.3 us
  Pallas kernels  59.9 us (98%)
  local copies, waits for them, and re-layouts  1.42 us (2%)
    pallas_call x1, Pallas kernels, local(): pl.pallas_call(kernel, out_shape=jax.ShapeDtypeStruct((REQUESTS, HALF), B...  59.9 us
    unnamed x1, local copies, waits for them, and re-layouts  1.42 us

profile of v4, /device:TPU:1, one launch (start us, length us, event | category | flops | bytes accessed | tf_op | source)
XLA Modules:
  0.0 61.3 jit_solution(4427301129723219043)
XLA Ops:
  0.0 59.9 %shard_map.100 = bf16[16,1536]{1,0:T(8,128)(2,1)} custom-call(bf16[16,3072]{1,0:T(8,128)(2,1)} %q_hbm.1, bf16[16,128,512]{2,1,0:T(8,128)(2,1)} %k_hbm.1, bf16[16,128,512]{2,1,0:T(8,128)(2,1)} %v_hbm.1, s32[16]{0:T(128)} %len_hbm.1, f32[1,3072]{1,0:T(1,128)} %bitcast.3, s32[2,16]{1,0:T(2,128)} %bitcast.4, f32[2,16]{1,0:T(2,128)} %bitcast.5, ...), custom_call_target="tpu_custom_call" | custom-call | flops 5000000000 | bytes 14000000 | tf_op jit(solution)/shard_map/pallas_call | solution.py:409
  59.9 1.4 %copy.12 = bf16[16,1536]{1,0:T(8,128)(2,1)} copy(bf16[16,1536]{1,0:T(8,128)(2,1)} %shard_map.100) | data formatting | bytes 98304

commit v5 on v4

--- a/solution.py
+++ b/solution.py
@@ -29,18 +29,18 @@
     ("across", 1, 1, -1), ("across", 0, 3, 1), ("across", 0, 3, -1), ("across", 1, 3, 1),
     ("across", 1, 3, -1), ("pass", 0, 0), ("pass", 1, 0), ("across", 0, 2, 1),
     ("across", 0, 2, -1), ("across", 1, 2, 1), ("across", 1, 2, -1), ("experts", 0),
-    ("down", 0, 0), ("down", 0, 1), ("pass", 0, 1), ("pass", 1, 1), ("pass", 0, 3),
+    ("pass", 0, 1), ("pass", 1, 1), ("down", 0, 0), ("down", 0, 1), ("pass", 0, 3),
     ("pass", 1, 3), ("pass", 0, 2), ("pass", 1, 2), ("experts", 3), ("down", 3, 0),
     ("down", 3, 1), ("direct", 1, 0, 2), ("direct", 0, 0, 2), ("direct", 1, 0, 1),
     ("direct", 0, 0, 1), ("direct", 1, 0, 3), ("direct", 0, 0, 3), ("direct", 1, 0, 0),
     ("direct", 0, 0, 0), ("direct", 1, 1, 2), ("direct", 0, 1, 2), ("direct", 1, 1, 1),
     ("direct", 0, 1, 1), ("direct", 1, 1, 3), ("direct", 0, 1, 3), ("direct", 1, 1, 0),
-    ("direct", 0, 1, 0), ("experts", 1), ("down", 1, 0), ("down", 1, 1), ("experts", 2),
-    ("down", 2, 0), ("opposite", 1, 0, 2), ("opposite", 0, 0, 2), ("opposite", 1, 0, 1),
-    ("opposite", 0, 0, 1), ("opposite", 1, 0, 3), ("opposite", 0, 0, 3), ("opposite", 1, 0, 0),
-    ("opposite", 0, 0, 0), ("down", 2, 1), ("opposite", 1, 1, 2), ("opposite", 0, 1, 2),
-    ("opposite", 1, 1, 1), ("opposite", 0, 1, 1), ("opposite", 1, 1, 3), ("opposite", 0, 1, 3),
-    ("opposite", 1, 1, 0), ("opposite", 0, 1, 0), ("sum", 1, 0, 2), ("sum", 0, 0, 2),
+    ("direct", 0, 1, 0), ("experts", 2), ("down", 2, 0), ("opposite", 1, 0, 2),
+    ("opposite", 0, 0, 2), ("opposite", 1, 0, 1), ("opposite", 0, 0, 1), ("opposite", 1, 0, 3),
+    ("opposite", 0, 0, 3), ("opposite", 1, 0, 0), ("opposite", 0, 0, 0), ("down", 2, 1),
+    ("opposite", 1, 1, 2), ("opposite", 0, 1, 2), ("opposite", 1, 1, 1), ("opposite", 0, 1, 1),
+    ("opposite", 1, 1, 3), ("opposite", 0, 1, 3), ("opposite", 1, 1, 0), ("opposite", 0, 1, 0),
+    ("experts", 1), ("down", 1, 0), ("down", 1, 1), ("sum", 1, 0, 2), ("sum", 0, 0, 2),
     ("sum", 1, 0, 1), ("sum", 0, 0, 1), ("sum", 1, 0, 3), ("sum", 0, 0, 3), ("sum", 1, 0, 0),
     ("sum", 0, 0, 0), ("sum", 1, 1, 2), ("sum", 0, 1, 2), ("sum", 1, 1, 1), ("sum", 0, 1, 1),
     ("sum", 1, 1, 3), ("sum", 0, 1, 3), ("sum", 1, 1, 0), ("sum", 0, 1, 0), ("line", 1, 0, 2),
@@ -75,7 +75,7 @@
     q_hbm, k_hbm, v_hbm, len_hbm, gain_hbm, ids_hbm, gates_hbm, wg_hbm, wu_hbm, wd_hbm,
     out_ref,
     q_buf, gain, ids, gates, k_buf, v_buf, wg, wu, wd, q_rows, s_rows, c_rows,
-    packed, landed, xs, hidden, parts, r1, r2, r3, back, home, table, lengths,
+    packed, landed, xs, hidden, parts, r1, r2, r3, back, home, table, chosen, lengths,
     local_sem, sent, z_recv, ag_recv, rs_recv, ret_recv,
 ):
     role = lax.axis_index("role")
@@ -94,9 +94,10 @@
         return (core, (z + step + 8) % 8, t)
 
     barrier = pltpu.get_barrier_semaphore()
-    partners = [at(0, a, step) for a in (0, 1) for step in (1, -1, 2)] + [at_z(0, 1 - role)]
-    for step in OFFSETS[1:]:
+    partners = []
+    for step in OFFSETS[:0:-1]:
         partners += [at_z(step, role), at_z(step, 1 - role)]
+    partners += [at(0, a, step) for a in (0, 1) for step in (2, 1, -1)] + [at_z(0, 1 - role)]
     for partner in partners:
         pl.semaphore_signal(barrier, inc=1, device_id=partner, device_id_type=MESH)
 
@@ -120,11 +121,12 @@
     ]
     small[0].start()
     small[1].start()
+    small[2].start()
     for kc, _ in loads:
         kc.start()
     for _, vc in loads:
         vc.start()
-    for copy in small[2:]:
+    for copy in small[3:]:
         copy.start()
 
     small[0].wait()
@@ -151,6 +153,20 @@
         )
     for wc in weight_loads:
         wc.start()
+    for copy in small[2:]:
+        copy.wait()
+    diagonal = iota((16, 16), 0) == iota((16, 16), 1)
+    first = jnp.concatenate([ids[0:1, :]] * 4, axis=1)
+    second = jnp.concatenate([ids[1:2, :]] * 4, axis=1)
+    row, col = iota((128, 64), 0), iota((128, 64), 1)
+    expert = (z + turn * offset_of(row // 16) + 8) % 8
+    hit = (first == expert) | (second == expert)
+    trow, tcol = iota((64, 64), 0), iota((64, 64), 1)
+    earlier = (trow // 16 == tcol // 16) & (trow % 16 < tcol % 16)
+    rank = dot(one_hot(hit), one_hot(earlier))
+    slot = ((row // 4) % 4 + 4 * role).astype(F32)
+    chosen[...] = one_hot(hit & (rank == slot) & (row % 4 == col // 16))
+
     scores = s_rows[...]
     raised = jnp.exp(scores - jnp.max(scores, axis=1, keepdims=True))
     s_rows[...] = raised / jnp.sum(raised, axis=1, keepdims=True)
@@ -163,8 +179,6 @@
         for j in range(1, KEY_VALUE_HEADS):
             own = jnp.where(group == j, mixed[:, j * HEAD_WIDTH : (j + 1) * HEAD_WIDTH], own)
         c_rows[r * QUERY_HEADS : (r + 1) * QUERY_HEADS, :] = own
-    for copy in small[2:]:
-        copy.wait()
     heads = [
         c_rows[pl.ds(h, REQUESTS, stride=QUERY_HEADS), :] for h in range(QUERY_HEADS)
     ]
@@ -181,32 +195,24 @@
         [jnp.concatenate(expert_in[6 * i : 6 * i + 6], axis=1) for i in range(4)], axis=0
     ).astype(BF16)
 
-    diagonal = iota((16, 16), 0) == iota((16, 16), 1)
-    first = jnp.concatenate([ids[0:1, :]] * 4, axis=1)
-    second = jnp.concatenate([ids[1:2, :]] * 4, axis=1)
-    row, col = iota((128, 64), 0), iota((128, 64), 1)
-    expert = (z + turn * offset_of(row // 16) + 8) % 8
-    hit = (first == expert) | (second == expert)
-    trow, tcol = iota((64, 64), 0), iota((64, 64), 1)
-    earlier = (trow // 16 == tcol // 16) & (trow % 16 < tcol % 16)
-    rank = dot(one_hot(hit), one_hot(earlier))
-    slot = ((row // 4) % 4 + 4 * role).astype(F32)
-    chosen = one_hot(hit & (rank == slot) & (row % 4 == col // 16))
-    packets = dot(chosen, stacked).astype(BF16)
-    packed[...] = packets.reshape(8, ROWS, QUARTER)
-
-    pl.semaphore_wait(barrier, len(partners))
-
     def landing(ref, sem):
         pltpu.make_async_copy(ref, ref, sem).wait()
 
-    for j in (1, 2, 3, 7, 5, 6, 4):
-        pltpu.make_async_remote_copy(
-            src_ref=packed.at[j], dst_ref=landed.at[j],
-            send_sem=sent.at[0], recv_sem=z_recv.at[j // 4],
-            device_id=at_z(turn * OFFSETS[j], role), device_id_type=MESH,
-        ).start()
-    landed[0] = packets[:ROWS]
+    def dispatch(w):
+        packets = dot(chosen[64 * w : 64 * w + 64], stacked).astype(BF16)
+        packed[4 * w : 4 * w + 4] = packets.reshape(4, ROWS, QUARTER)
+        if w == 0:
+            landed[0] = packets[:ROWS]
+            pl.semaphore_wait(barrier, len(partners))
+        for j in ((1, 2, 3), (7, 5, 6, 4))[w]:
+            pltpu.make_async_remote_copy(
+                src_ref=packed.at[j], dst_ref=landed.at[j],
+                send_sem=sent.at[0], recv_sem=z_recv.at[w],
+                device_id=at_z(turn * OFFSETS[j], role), device_id_type=MESH,
+            ).start()
+
+    dispatch(0)
+    dispatch(1)
 
     def block(ref, w, u, v):
         return ref.at[pl.ds((v * 8 + w * 4 + u) * ROWS, ROWS), :]
@@ -435,6 +441,7 @@
             pltpu.VMEM((16, ROWS, EIGHTH), BF16),
             pltpu.VMEM((16, ROWS, EIGHTH), BF16),
             pltpu.VMEM((128, 256), BF16),
+            pltpu.VMEM((128, 64), BF16),
             pltpu.SMEM((REQUESTS,), jnp.int32),
             dma((16,)), dma((4,)), dma((2,)), dma((16,)), dma((36,)), dma((2,)),
         ],

time: 61.4 us -> 61.2 us (level)
  no operation moved by 1% of the time
where the time goes in v5:
time: 61.2 us; the launch traced here: 61.1 us
  Pallas kernels  59.6 us (97%)
  local copies, waits for them, and re-layouts  1.42 us (2%)
    pallas_call x1, Pallas kernels, local(): pl.pallas_call(kernel, out_shape=jax.ShapeDtypeStruct((REQUESTS, HALF), B...  59.6 us
    unnamed x1, local copies, waits for them, and re-layouts  1.42 us

profile of v5, /device:TPU:1, one launch (start us, length us, event | category | flops | bytes accessed | tf_op | source)
XLA Modules:
  0.0 61.1 jit_solution(9514532716033519487)
XLA Ops:
  0.0 59.6 %shard_map.100 = bf16[16,1536]{1,0:T(8,128)(2,1)} custom-call(bf16[16,3072]{1,0:T(8,128)(2,1)} %q_hbm.1, bf16[16,128,512]{2,1,0:T(8,128)(2,1)} %k_hbm.1, bf16[16,128,512]{2,1,0:T(8,128)(2,1)} %v_hbm.1, s32[16]{0:T(128)} %len_hbm.1, f32[1,3072]{1,0:T(1,128)} %bitcast.3, s32[2,16]{1,0:T(2,128)} %bitcast.4, f32[2,16]{1,0:T(2,128)} %bitcast.5, ...), custom_call_target="tpu_custom_call" | custom-call | flops 5000000000 | bytes 14000000 | tf_op jit(solution)/shard_map/pallas_call | solution.py:415
  59.6 1.4 %copy.12 = bf16[16,1536]{1,0:T(8,128)(2,1)} copy(bf16[16,1536]{1,0:T(8,128)(2,1)} %shard_map.100) | data formatting | bytes 98304
